TPU v7x, 32 devices: a whole 2x2x4 slice. The times are simulated.
32 devices in a mesh: slab: 2 (over y), col: 4 (over z), row: 2 (over x), ch: 2 (over core).
Axes of the slice: x: 2, y: 2, z: 4, core: 2. Of those that a mesh axis runs over, the one named last changes fastest.
Arguments:
- left_feat: bfloat16 [128, 128, 1024], P(('slab', 'row'), 'ch', 'col'), parts along dimension 0, may hold values from -512 to 512
- right_feat: bfloat16 [128, 128, 1024], P(('slab', 'row'), 'ch', 'col'), parts along dimension 0, may hold values from -12 to 12
- offsets: int32 [8], P(('slab', 'col')), parts along dimension 0, may hold values from 0 to 256, as said below
- valid: int32 [128, 1024], P(('slab', 'row'), ('col', 'ch')), parts along dimension 0, may hold values 0 or 1
- w_first: float32 [3, 3, 32, 2], replicated, may hold values from -1.5 to 1.5
- w_middle: float32 [3, 3, 32, 32], replicated, may hold values from -0.375 to 0.375
- w_last: float32 [3, 3, 1, 32], replicated, may hold values from -0.375 to 0.375
- grad_out: float32 [128, 1024], P(('slab', 'row'), ('col', 'ch')), parts along dimension 0, may hold values from -6 to 6
Outputs:
- refined: float32 [128, 1024], P(('slab', 'row'), ('col', 'ch')), parts along dimension 0
- grad_left: bfloat16 [128, 128, 1024], P(('slab', 'row'), 'ch', 'col'), parts along dimension 0
- grad_right: bfloat16 [128, 128, 1024], P(('slab', 'row'), 'ch', 'col'), parts along dimension 0
There are 2 independent parts, one for each index of `slab`. A program takes and returns all parts, laid end to end along the dimension named above; an argument that names none is the same for every part. Nothing has to cross between parts.
Inputs may be any that keep to these rules, and one draw needn't show every extreme that they name: `offsets`: the largest tile offset is exactly 256 in every draw.
All inputs are finite; a program needn't handle non-finite values. No bound on the sum of `valid` on one device may be relied on, other than what follows from the above.
Results may differ from a plain program's by a relative error of at most 0.005.
Values may be sent and summed in bfloat16 or wider, within the bound.
A program may use at most 128 MiB of HBM per device.

v0:
```python
import functools
import math

import jax
import jax.numpy as jnp
from jax import lax
from jax.experimental import pallas as pl
from jax.experimental.pallas import tpu as pltpu
from jax.sharding import PartitionSpec as P

FEAT = 128
DISP = 256
HALO = 4
LANES = 128
VMEM = 56 * 1024 * 1024
F32, BF16 = jnp.float32, jnp.bfloat16


def from_behind(value, axis, steps):
    count = lax.axis_size(axis)
    first, last = (max(0, -steps), min(count, count - steps))
    return lax.ppermute(value, axis, [(source, source + steps) for source in range(first, last)])


def with_halo(shard, axis, dim, width):
    length = shard.shape[dim]
    before = from_behind(lax.slice_in_dim(shard, length - width, length, axis=dim), axis, 1)
    after = from_behind(lax.slice_in_dim(shard, 0, width, axis=dim), axis, -1)
    return jnp.concatenate([before, shard, after], axis=dim)


def band_of(offset, window_refs, tile):
    window = jnp.concatenate([ref[0] for ref in window_refs], axis=1).astype(F32)
    span = window.shape[1]
    start = span - tile - DISP - offset
    return pltpu.roll(window, span - start, 1)[:, : tile + DISP].astype(BF16)


def skew_out(products):
    tile, span = products.shape
    row_ids = lax.broadcasted_iota(jnp.int32, products.shape, 0)
    for bit in (1, 2, 4):
        products = jnp.where((row_ids & bit) != 0, pltpu.roll(products, span - bit, 1), products)
    pieces = [
        pltpu.roll(products[base : base + 8], span - base - 1, 1)[:, :DISP]
        for base in range(0, tile, 8)
    ]
    return jnp.concatenate(pieces, axis=0)


def skew_in(values, span):
    tile = values.shape[0]
    padded = jnp.concatenate([values, jnp.zeros((tile, span - DISP), values.dtype)], axis=1)
    pieces = [pltpu.roll(padded[base : base + 8], base + 1, 1) for base in range(0, tile, 8)]
    skewed = jnp.concatenate(pieces, axis=0)
    row_ids = lax.broadcasted_iota(jnp.int32, skewed.shape, 0)
    for bit in (1, 2, 4):
        skewed = jnp.where((row_ids & bit) != 0, pltpu.roll(skewed, bit, 1), skewed)
    return skewed


def levels_of(shape):
    return (DISP - 1 - lax.broadcasted_iota(jnp.int32, shape, 1)).astype(F32) / DISP


def cost_kernel(offset_ref, left_ref, far_ref, mid_ref, near_ref, probs_ref, stats_ref):
    row = pl.program_id(0)
    tile = left_ref.shape[2]
    band = band_of(offset_ref[0], (far_ref, mid_ref, near_ref), tile)
    products = lax.dot_general(
        left_ref[0], band, (((0,), (0,)), ((), ())), preferred_element_type=F32
    )
    scores = skew_out(products) / math.sqrt(FEAT)
    exps = jnp.exp(scores - jnp.max(scores, axis=1, keepdims=True))
    probs = exps / jnp.sum(exps, axis=1, keepdims=True)
    levels = levels_of(probs.shape)
    mean = jnp.sum(probs * levels, axis=1, keepdims=True)
    spread = jnp.sum(probs * (levels - mean) ** 2, axis=1, keepdims=True)
    probs_ref[0] = probs
    lanes = lax.broadcasted_iota(jnp.int32, stats_ref.shape, 1)

    @pl.when(row == 0)
    def _():
        stats_ref[...] = jnp.zeros_like(stats_ref)

    stats_ref[...] = jnp.where(
        lanes == row, mean, jnp.where(lanes == row + LANES // 2, spread, stats_ref[...])
    )


def grad_kernel(
    offset_ref, left_ref, far_ref, mid_ref, near_ref, probs_ref, stats_ref, cots_ref,
    left_out, far_out, mid_out, near_out,
):
    row = pl.program_id(0)
    tile = left_ref.shape[2]
    offset = offset_ref[0]
    band = band_of(offset, (far_ref, mid_ref, near_ref), tile)
    lanes = lax.broadcasted_iota(jnp.int32, stats_ref.shape, 1)

    def column(ref, index):
        return jnp.sum(jnp.where(lanes == index, ref[...], 0.0), axis=1, keepdims=True)

    mean = column(stats_ref, row)
    spread = column(stats_ref, row + LANES // 2)
    cot_mean = column(cots_ref, row)
    cot_spread = column(cots_ref, row + LANES // 2)
    probs = probs_ref[0]
    apart = levels_of(probs.shape) - mean
    grad_scores = probs * (cot_mean * apart + cot_spread * (apart * apart - spread))
    grad_cost = (grad_scores / math.sqrt(FEAT)).astype(BF16).astype(F32)
    skewed = skew_in(grad_cost, tile + DISP).astype(BF16)
    left_grad = lax.dot_general(
        band, skewed, (((1,), (1,)), ((), ())), preferred_element_type=F32
    )
    left_out[0] = left_grad.astype(BF16)
    right_grad = jnp.dot(left_ref[0], skewed, preferred_element_type=F32)
    span = 3 * tile
    padded = jnp.concatenate(
        [right_grad, jnp.zeros((right_grad.shape[0], span - tile - DISP), F32)], axis=1
    )
    moved = pltpu.roll(padded, span - tile - DISP - offset, 1)
    far_out[0] = moved[:, :tile].astype(BF16)
    mid_out[0] = moved[:, tile : 2 * tile]
    near_out[0] = moved[:, 2 * tile :]


def split_halves(values):
    upper = values.astype(BF16)
    return upper, (values - upper.astype(F32)).astype(BF16)


def weight_side(matrix, rows, depth):
    padded = jnp.pad(matrix, ((0, rows - matrix.shape[0]), (0, depth - matrix.shape[1])))
    upper, lower = split_halves(padded)
    return jnp.concatenate([upper, upper, lower], axis=1)


def field_side(values):
    upper, lower = split_halves(values)
    return jnp.concatenate([upper, lower, upper], axis=0)


def refine_kernel(
    stride, fields_ref, first_ref, middle_ref, last_ref, last_back_ref, middle_back_ref,
    first_back_ref, out_ref, slope_one, slope_two, packed, spread_out,
):
    cells = fields_ref.shape[1]
    chans = slope_one.shape[0]
    taps = [(a - 1) * stride + (b - 1) for a in range(3) for b in range(3)]

    def ahead(values, steps):
        return values if steps == 0 else pltpu.roll(values, -steps % cells, 1)

    def gather(rows, sign, depth):
        parts = [ahead(rows, sign * tap) for tap in taps]
        count = sum(part.shape[0] for part in parts)
        parts.append(jnp.zeros((depth - count, cells), F32))
        return jnp.concatenate(parts, axis=0)

    def product(weights_ref, values):
        return jnp.dot(weights_ref[...], field_side(values), preferred_element_type=F32)

    def scatter(rows_of, sign):
        total = None
        for index, tap in enumerate(taps):
            part = ahead(rows_of(index), sign * tap)
            total = part if total is None else total + part
        return total

    def silu_parts(values):
        sig = 1.0 / (1.0 + jnp.exp(-values))
        return values * sig, sig * (1.0 + values * (1.0 - sig))

    def middle(weights_ref, sign):
        spread_out[...] = jnp.dot(weights_ref[...], packed[...], preferred_element_type=F32)
        return scatter(lambda index: spread_out[index * chans : (index + 1) * chans], sign)

    inside = fields_ref[3:4]
    hidden, slope = silu_parts(product(first_ref, gather(fields_ref[0:2], 1, chans)))
    slope_one[...] = slope * inside
    packed[...] = field_side(hidden * inside)
    hidden, slope = silu_parts(middle(middle_ref, 1))
    slope_two[...] = slope * inside
    rows = product(last_ref, hidden * inside)
    out_ref[0:1] = scatter(lambda index: rows[index : index + 1], 1)
    grad_two = product(last_back_ref, gather(fields_ref[2:3], -1, chans)) * slope_two[...]
    packed[...] = field_side(grad_two)
    grad_one = middle(middle_back_ref, -1) * slope_one[...]
    rows = product(first_back_ref, grad_one)
    out_ref[1:3] = scatter(lambda index: rows[2 * index : 2 * index + 2], -1)
    out_ref[3:8] = jnp.zeros((5, cells), F32)


def refine(fields, w_first, w_middle, w_last):
    count, rows, cols = fields.shape
    cells = rows * cols
    padded_cells = -(-cells // 256) * 256
    flat = jnp.pad(fields.reshape(count, cells), ((0, 8 - count), (0, padded_cells - cells)))
    chans = w_middle.shape[2]
    first = weight_side(w_first.transpose(2, 0, 1, 3).reshape(chans, -1), chans, chans)
    middle = weight_side(w_middle.reshape(-1, chans), 9 * chans, chans)
    last = weight_side(w_last.reshape(9, chans), 16, chans)
    last_back = weight_side(w_last.reshape(9, chans).T, chans, chans)
    middle_back = weight_side(w_middle.transpose(0, 1, 3, 2).reshape(-1, chans), 9 * chans, chans)
    first_back = weight_side(w_first.transpose(0, 1, 3, 2).reshape(-1, chans), chans, chans)
    out = pl.pallas_call(
        functools.partial(refine_kernel, cols),
        out_shape=jax.ShapeDtypeStruct((8, padded_cells), F32),
        in_specs=[pl.BlockSpec(memory_space=pltpu.VMEM)] * 7,
        out_specs=pl.BlockSpec(memory_space=pltpu.VMEM),
        scratch_shapes=[
            pltpu.VMEM((chans, padded_cells), F32),
            pltpu.VMEM((chans, padded_cells), F32),
            pltpu.VMEM((3 * chans, padded_cells), BF16),
            pltpu.VMEM((9 * chans, padded_cells), F32),
        ],
        compiler_params=pltpu.CompilerParams(vmem_limit_bytes=VMEM),
        name="refine",
    )(flat, first, middle, last, last_back, middle_back, first_back)
    return out[:3, :cells].reshape(3, rows, cols)


def row_block(array):
    return pl.BlockSpec((1,) + array.shape[1:], lambda row: (row, 0, 0))


def whole_block(shape):
    return pl.BlockSpec(shape, lambda row: (0, 0))


def match(offsets, left, window):
    rows, _, tile = left.shape
    probs = jax.ShapeDtypeStruct((rows, tile, DISP), F32)
    stats = jax.ShapeDtypeStruct((tile, LANES), F32)
    return pl.pallas_call(
        cost_kernel,
        grid=(rows,),
        in_specs=[pl.BlockSpec(memory_space=pltpu.SMEM), row_block(left)]
        + [row_block(part) for part in window],
        out_specs=[row_block(probs), whole_block(stats.shape)],
        out_shape=[probs, stats],
        compiler_params=pltpu.CompilerParams(vmem_limit_bytes=VMEM),
        name="match",
    )(offsets, left, *window)


def match_grads(offsets, left, window, probs, stats, cots):
    rows, feats, tile = left.shape
    narrow = jax.ShapeDtypeStruct((rows, feats, tile), BF16)
    wide = jax.ShapeDtypeStruct((rows, feats, tile), F32)
    return pl.pallas_call(
        grad_kernel,
        grid=(rows,),
        in_specs=[pl.BlockSpec(memory_space=pltpu.SMEM), row_block(left)]
        + [row_block(part) for part in window]
        + [row_block(probs), whole_block(stats.shape), whole_block(cots.shape)],
        out_specs=[row_block(left)] * 4,
        out_shape=[narrow, narrow, wide, wide],
        compiler_params=pltpu.CompilerParams(vmem_limit_bytes=VMEM),
        name="match_grads",
    )(offsets, left, *window, probs, stats, cots)


def to_rows(array, rows_dim, other_dim):
    return lax.all_to_all(array, "ch", rows_dim, other_dim, tiled=True)


def shards(left_feat, right_feat, offsets, valid, w_first, w_middle, w_last, grad_out):
    near = to_rows(right_feat, 0, 1)
    mid = from_behind(near, "col", 1)
    left = to_rows(left_feat, 0, 1)
    keep_cols = valid.astype(F32)
    planes = to_rows(jnp.stack([keep_cols, grad_out * keep_cols]), 1, 2)
    keep, grad_top = planes[0], planes[1]
    far = from_behind(mid, "col", 1)
    window = (far, mid, near)
    probs, stats = match(offsets, left, window)
    rows, cols = keep.shape
    flipped = stats.T
    coarse = offsets[0].astype(F32) / DISP + flipped[:rows]
    spread = flipped[LANES // 2 : LANES // 2 + rows]
    fields = jnp.stack([coarse * keep, spread * keep, grad_top])
    fields = with_halo(fields, ("row", "ch"), 1, HALO)
    fields = with_halo(fields, "col", 2, HALO)
    row_at = lax.axis_index(("row", "ch")) * rows - HALO + jnp.arange(rows + 2 * HALO)
    col_at = lax.axis_index("col") * cols - HALO + jnp.arange(cols + 2 * HALO)
    row_in = (row_at >= 0) & (row_at < rows * lax.axis_size(("row", "ch")))
    col_in = (col_at >= 0) & (col_at < cols * lax.axis_size("col"))
    inside = (row_in[:, None] & col_in[None, :]).astype(F32)
    results = refine(jnp.concatenate([fields, inside[None]]), w_first, w_middle, w_last)
    results = results[:, HALO : HALO + rows, HALO : HALO + cols]
    refined = keep * (coarse + results[0])
    gap = jnp.zeros((LANES // 2 - rows, cols), F32)
    cots = jnp.concatenate(
        [grad_top + results[1] * keep, gap, results[2] * keep, gap]
    ).T
    grad_left, far_grad, mid_grad, near_grad = match_grads(
        offsets, left, window, probs, stats, cots
    )
    carried = from_behind(far_grad, "col", -1)
    carried = from_behind((mid_grad + carried.astype(F32)).astype(BF16), "col", -1)
    grad_right = (near_grad + carried.astype(F32)).astype(BF16)
    return (
        to_rows(refined, 1, 0),
        to_rows(grad_left, 1, 0),
        to_rows(grad_right, 1, 0),
    )


def solution(mesh):
    placed = (
        P(("slab", "row"), "ch", "col"),
        P(("slab", "row"), "ch", "col"),
        P(("slab", "col")),
        P(("slab", "row"), ("col", "ch")),
        P(),
        P(),
        P(),
        P(("slab", "row"), ("col", "ch")),
    )
    return jax.shard_map(
        shards,
        mesh=mesh,
        in_specs=placed,
        out_specs=(
            P(("slab", "row"), ("col", "ch")),
            P(("slab", "row"), "ch", "col"),
            P(("slab", "row"), "ch", "col"),
        ),
        check_vma=False,
    )
```

profile of v0, /device:TPU:0, one launch (start us, length us, event | category | flops | bytes accessed | tf_op | source)
XLA Modules:
  0.0 200.8 jit_solution(15931118245489900910)
XLA Ops:
  0.7 3.7 %all-to-all-start.2 = ((bf16[32,64,256]{2,1,0:T(8,128)(2,1)}), bf16[32,64,256]{2,1,0:T(8,128)(2,1)S(1)}, u32[]{:S(2)}, u32[]{:S(2)}) async-start(bf16[32,64,256]{2,1,0:T(8,128)(2,1)} %param.9), calls=%async_computation.2 | async-start | bytes 2097152 | tf_op jit(solution)/shard_map/all_to_all | solution.py:266
  5.1 1.4 all-to-all-done.2
  6.5 3.3 %all-to-all-start = ((f32[2,32,128]{2,0,1:T(2,128)}), f32[2,32,128]{2,0,1:T(2,128)S(1)}, u32[]{:S(2)}, u32[]{:S(2)}) async-start(f32[2,32,128]{2,0,1:T(2,128)} %pad_maximum_fusion.4), calls=%async_computation | async-start | bytes 65536 | tf_op jit(solution)/shard_map/all_to_all | solution.py:266
  9.9 5.0 %collective-permute-start = (bf16[16,128,256]{2,1,0:T(8,128)(2,1)S(1)}, bf16[16,128,256]{2,1,0:T(8,128)(2,1)S(1)}, u32[]{:S(2)}, u32[]{:S(2)}) collective-permute-start(bf16[16,128,256]{2,1,0:T(8,128)(2,1)S(1)} %bitcast.74), channel_id=1, source_target_pairs={{0,4},{4,8},{8,12},{1,5},{5,9},{9,13},{2,6},{6,10},{10,14},{3,7},{... | collective-permute-start | bytes 3145736 | tf_op jit(solution)/shard_map/ppermute | solution.py:22
  20.5 3.6 %all-to-all-start.1 = ((bf16[32,64,256]{2,1,0:T(8,128)(2,1)}), bf16[32,64,256]{2,1,0:T(8,128)(2,1)S(1)}, u32[]{:S(2)}, u32[]{:S(2)}) async-start(bf16[32,64,256]{2,1,0:T(8,128)(2,1)} %param.8), calls=%async_computation.1 | async-start | bytes 2097152 | tf_op jit(solution)/shard_map/all_to_all | solution.py:266
  24.1 1.6 copy.35
  26.8 1.4 pad_maximum_fusion.10.first_back_ref
  28.2 1.5 pad_maximum_fusion.8
  31.5 1.4 and.44
  34.2 1.4 and.47
  39.1 3.5 %collective-permute-start.1 = (bf16[16,128,256]{2,1,0:T(8,128)(2,1)S(1)}, bf16[16,128,256]{2,1,0:T(8,128)(2,1)S(1)}, u32[]{:S(2)}, u32[]{:S(2)}) collective-permute-start(bf16[16,128,256]{2,1,0:T(8,128)(2,1)S(1)} %collective-permute-done.mid_ref), channel_id=1, source_target_pairs={{0,4},{4,8},{8,12},{1,5},{5,9},{9,13},{2,6},{6,10},{10,14},{3,7},{... | collective-permute-start | bytes 3145736 | tf_op jit(solution)/shard_map/ppermute | solution.py:22
  43.3 22.2 %collective-permute-done.1.far_ref = bf16[16,128,256]{2,1,0:T(8,128)(2,1)S(1)} collective-permute-done((bf16[16,128,256]{2,1,0:T(8,128)(2,1)S(1)}, bf16[16,128,256]{2,1,0:T(8,128)(2,1)S(1)}, u32[]{:S(2)}, u32[]{:S(2)}) %collective-permute-start.1) | collective-permute-done | bytes 1048608 | tf_op jit(solution)/shard_map/ppermute | solution.py:22
  66.5 22.0 %match.1 = (f32[16,256,256]{2,1,0:T(8,128)}, f32[256,128]{1,0:T(8,128)}) custom-call(s32[1]{0:T(128)S(6)} %copy.58.offset_ref, bf16[16,128,256]{2,1,0:T(8,128)(2,1)} %bitcast.77, bf16[16,128,256]{2,1,0:T(8,128)(2,1)} %copy-done.2, bf16[16,128,256]{2,1,0:T(8,128)(2,1)} %copy-done.1, bf16[16,128,256]{2,1,0:T(8,128)(2,1)} %bitcast.75), custom_call_target="tpu_custom_call" | custom-call | tf_op jit(solution)/shard_map/match/pallas_call | solution.py:236
  91.1 3.0 %collective-permute-start.2 = (f32[3,4,256]{2,1,0:T(4,128)S(1)}, f32[3,4,256]{2,1,0:T(4,128)S(1)}, u32[]{:S(2)}, u32[]{:S(2)}) collective-permute-start(f32[3,4,256]{2,1,0:T(4,128)S(1)} %get-tuple-element.27), channel_id=1, source_target_pairs={{0,1},{1,2},{2,3},{4,5},{5,6},{6,7},{8,9},{9,10},{10,11},{12,13},{... | collective-permute-start | bytes 36872 | tf_op jit(solution)/shard_map/ppermute | solution.py:22
  96.4 5.2 %collective-permute-start.4 = (f32[3,24,4]{2,1,0:T(8,128)S(1)}, f32[3,24,4]{2,1,0:T(8,128)S(1)}, u32[]{:S(2)}, u32[]{:S(2)}) collective-permute-start(f32[3,24,4]{2,1,0:T(8,128)S(1)} %get-tuple-element.25), channel_id=1, source_target_pairs={{0,4},{4,8},{8,12},{1,5},{5,9},{9,13},{2,6},{6,10},{10,14},{3,7},{... | collective-permute-start | bytes 3464 | tf_op jit(solution)/shard_map/ppermute | solution.py:22
  104.1 9.7 %refine.1 = f32[8,6400]{1,0:T(8,128)} custom-call(f32[8,6400]{1,0:T(8,128)} %select_maximum_fusion.fields_ref, bf16[32,96]{1,0:T(8,128)(2,1)} %get-tuple-element.31.first_ref, bf16[288,96]{1,0:T(8,128)(2,1)} %get-tuple-element.29.middle_ref, bf16[16,96]{1,0:T(8,128)(2,1)} %pad_maximum_fusion.11.last_ref, bf16[32,96]{1,0:T(8,128)(2,1)} %get-tuple-element.32.last_back_ref, ...), custom_call_target="tpu_custom_call" | custom-call | tf_op jit(solution)/shard_map/refine/pallas_call | solution.py:207
  116.2 20.5 %match_grads.1 = (bf16[16,128,256]{2,1,0:T(8,128)(2,1)}, bf16[16,128,256]{2,1,0:T(8,128)(2,1)}, f32[16,128,256]{2,1,0:T(8,128)}, f32[16,128,256]{2,1,0:T(8,128)}) custom-call(s32[1]{0:T(128)S(6)} %copy.58.offset_ref, bf16[16,128,256]{2,1,0:T(8,128)(2,1)} %bitcast.78, bf16[16,128,256]{2,1,0:T(8,128)(2,1)} %copy-done.2, bf16[16,128,256]{2,1,0:T(8,128)(2,1)} %copy-done.1, ...), custom_call_target="tpu_custom_call" | custom-call | tf_op jit(solution)/shard_map/match_grads/pallas_call | solution.py:252
  138.0 26.7 %collective-permute-done.6 = bf16[16,128,256]{2,1,0:T(8,128)(2,1)S(1)} collective-permute-done((bf16[16,128,256]{2,1,0:T(8,128)(2,1)}, bf16[16,128,256]{2,1,0:T(8,128)(2,1)S(1)}, u32[]{:S(2)}, u32[]{:S(2)}) %collective-permute-start.6) | collective-permute-done | bytes 1048608 | tf_op jit(solution)/shard_map/ppermute | solution.py:22
  164.8 2.0 add_convert_fusion.1
  168.1 3.7 %all_to_all.106 = f32[16,2,128]{2,0,1:T(8,128)S(1)} all-to-all(f32[16,2,128]{2,0,1:T(8,128)S(1)} %copy.45), channel_id=1, replica_groups=mesh['slab'=2,'col'=4,'row'=2,'ch'=2] {'ch'}, dimensions={1} | all-to-all | bytes 32768 | tf_op jit(solution)/shard_map/all_to_all | solution.py:266
  172.4 4.7 %all_to_all.107 = bf16[16,128,256]{2,0,1:T(8,128)(2,1)S(1)} all-to-all(bf16[16,128,256]{2,0,1:T(8,128)(2,1)S(1)} %copy.48), channel_id=1, replica_groups=mesh['slab'=2,'col'=4,'row'=2,'ch'=2] {'ch'}, dimensions={1} | all-to-all | bytes 2097152 | tf_op jit(solution)/shard_map/all_to_all | solution.py:266
  177.1 1.3 copy.49
  178.4 14.9 %collective-permute-done.7 = bf16[16,128,256]{2,1,0:T(8,128)(2,1)S(1)} collective-permute-done((bf16[16,128,256]{2,1,0:T(8,128)(2,1)S(1)}, bf16[16,128,256]{2,1,0:T(8,128)(2,1)S(1)}, u32[]{:S(2)}, u32[]{:S(2)}) %collective-permute-start.7) | collective-permute-done | bytes 1048608 | tf_op jit(solution)/shard_map/ppermute | solution.py:22
  194.3 4.6 %all_to_all.108 = bf16[16,128,256]{2,0,1:T(8,128)(2,1)S(1)} all-to-all(bf16[16,128,256]{2,0,1:T(8,128)(2,1)S(1)} %copy.50), channel_id=1, replica_groups=mesh['slab'=2,'col'=4,'row'=2,'ch'=2] {'ch'}, dimensions={1} | all-to-all | bytes 2097152 | tf_op jit(solution)/shard_map/all_to_all | solution.py:266
  (100 shorter events, 30.7 us)
Async XLA Ops:
  0.6 3.8 %copy-start.13 = (f32[32,128]{1,0:T(8,128)S(1)}, f32[32,128]{1,0:T(8,128)}, u32[]{:S(2)}) copy-start(f32[32,128]{1,0:T(8,128)} %param.15) | copy-start | bytes 49156
  0.7 14.2 %copy-start.12 = (f32[3,3,32,2]{2,3,1,0:T(2,128)S(1)}, f32[3,3,32,2]{2,3,1,0:T(2,128)}, u32[]{:S(2)}) copy-start(f32[3,3,32,2]{2,3,1,0:T(2,128)} %param.12) | copy-start | bytes 6916
  0.7 15.6 %copy-start.15 = (f32[3,3,1,32]{3,2,1,0:T(1,128)S(1)}, f32[3,3,1,32]{3,2,1,0:T(1,128)}, u32[]{:S(2)}) copy-start(f32[3,3,1,32]{3,2,1,0:T(1,128)} %param.14) | copy-start | bytes 3460
  0.7 5.8 %all-to-all-start.2 = ((bf16[32,64,256]{2,1,0:T(8,128)(2,1)}), bf16[32,64,256]{2,1,0:T(8,128)(2,1)S(1)}, u32[]{:S(2)}, u32[]{:S(2)}) async-start(bf16[32,64,256]{2,1,0:T(8,128)(2,1)} %param.9), calls=%async_computation.2 | async-start | bytes 2097152 | tf_op jit(solution)/shard_map/all_to_all | solution.py:266
  6.5 13.4 %all-to-all-start = ((f32[2,32,128]{2,0,1:T(2,128)}), f32[2,32,128]{2,0,1:T(2,128)S(1)}, u32[]{:S(2)}, u32[]{:S(2)}) async-start(f32[2,32,128]{2,0,1:T(2,128)} %pad_maximum_fusion.4), calls=%async_computation | async-start | bytes 65536 | tf_op jit(solution)/shard_map/all_to_all | solution.py:266
  9.9 28.2 %copy-start = (bf16[2,16,64,256]{3,2,0,1:T(8,128)(2,1)}, bf16[2,16,64,256]{3,2,0,1:T(8,128)(2,1)S(1)}, u32[]{:S(2)}) copy-start(bf16[2,16,64,256]{3,2,0,1:T(8,128)(2,1)S(1)} %copy.37) | copy-start | bytes 3145732
  9.9 29.2 %collective-permute-start = (bf16[16,128,256]{2,1,0:T(8,128)(2,1)S(1)}, bf16[16,128,256]{2,1,0:T(8,128)(2,1)S(1)}, u32[]{:S(2)}, u32[]{:S(2)}) collective-permute-start(bf16[16,128,256]{2,1,0:T(8,128)(2,1)S(1)} %bitcast.74), channel_id=1, source_target_pairs={{0,4},{4,8},{8,12},{1,5},{5,9},{9,13},{2,6},{6,10},{10,14},{3,7},{... | collective-permute-start | bytes 3145736 | tf_op jit(solution)/shard_map/ppermute | solution.py:22
  16.3 9.5 %copy-start.9 = (f32[9,32]{1,0:T(8,128)}, f32[9,32]{1,0:T(8,128)S(1)}, u32[]{:S(2)}) copy-start(f32[9,32]{1,0:T(8,128)S(1)} %reshape.86) | copy-start | bytes 3460
  20.5 16.4 %all-to-all-start.1 = ((bf16[32,64,256]{2,1,0:T(8,128)(2,1)}), bf16[32,64,256]{2,1,0:T(8,128)(2,1)S(1)}, u32[]{:S(2)}, u32[]{:S(2)}) async-start(bf16[32,64,256]{2,1,0:T(8,128)(2,1)} %param.8), calls=%async_computation.1 | async-start | bytes 2097152 | tf_op jit(solution)/shard_map/all_to_all | solution.py:266
  24.1 13.9 %copy-start.5 = (f32[3,3,32,32]{3,2,1,0:T(8,128)S(1)}, f32[3,3,32,32]{3,2,1,0:T(8,128)}, u32[]{:S(2)}) copy-start(f32[3,3,32,32]{3,2,1,0:T(8,128)} %param.13) | copy-start | bytes 110596
  39.1 26.5 %copy-start.1 = (bf16[16,128,256]{2,1,0:T(8,128)(2,1)}, bf16[16,128,256]{2,1,0:T(8,128)(2,1)S(1)}, u32[]{:S(2)}) copy-start(bf16[16,128,256]{2,1,0:T(8,128)(2,1)S(1)} %collective-permute-done.mid_ref) | copy-start | bytes 3145732
  39.1 26.5 %collective-permute-start.1 = (bf16[16,128,256]{2,1,0:T(8,128)(2,1)S(1)}, bf16[16,128,256]{2,1,0:T(8,128)(2,1)S(1)}, u32[]{:S(2)}, u32[]{:S(2)}) collective-permute-start(bf16[16,128,256]{2,1,0:T(8,128)(2,1)S(1)} %collective-permute-done.mid_ref), channel_id=1, source_target_pairs={{0,4},{4,8},{8,12},{1,5},{5,9},{9,13},{2,6},{6,10},{10,14},{3,7},{... | collective-permute-start | bytes 3145736 | tf_op jit(solution)/shard_map/ppermute | solution.py:22
  66.5 23.3 %copy-start.7 = (f32[1,16,256]{2,1,0:T(8,128)S(1)}, f32[1,16,256]{2,1,0:T(8,128)}, u32[]{:S(2)}) copy-start(f32[1,16,256]{2,1,0:T(8,128)} %copy.52) | copy-start | bytes 49156
  66.5 27.7 %copy-start.10 = (f32[9,32]{1,0:T(8,128)S(1)}, f32[9,32]{1,0:T(8,128)}, u32[]{:S(2)}) copy-start(f32[9,32]{1,0:T(8,128)} %copy-done.9) | copy-start | bytes 3460
  66.5 35.1 %copy-start.14 = (bf16[16,32]{1,0:T(8,128)(2,1)S(1)}, bf16[16,32]{1,0:T(8,128)(2,1)}, u32[]{:S(2)}) copy-start(bf16[16,32]{1,0:T(8,128)(2,1)} %subtract_convert_fusion.2) | copy-start | bytes 3076
  88.5 26.8 %copy-start.3 = (f32[256,128]{1,0:T(8,128)S(1)}, f32[256,128]{1,0:T(8,128)}, u32[]{:S(2)}) copy-start(f32[256,128]{1,0:T(8,128)} %get-tuple-element.9.stats_ref) | copy-start | bytes 393220
  89.8 4.4 %collective-permute-start.3 = (f32[3,4,256]{2,1,0:T(4,128)S(1)}, f32[3,4,256]{2,1,0:T(4,128)S(1)}, u32[]{:S(2)}, u32[]{:S(2)}) collective-permute-start(f32[3,4,256]{2,1,0:T(4,128)S(1)} %get-tuple-element.28), channel_id=1, source_target_pairs={{1,0},{2,1},{3,2},{5,4},{6,5},{7,6},{9,8},{10,9},{11,10},{13,12},{... | collective-permute-start | bytes 36872 | tf_op jit(solution)/shard_map/ppermute | solution.py:22
  91.1 3.9 %collective-permute-start.2 = (f32[3,4,256]{2,1,0:T(4,128)S(1)}, f32[3,4,256]{2,1,0:T(4,128)S(1)}, u32[]{:S(2)}, u32[]{:S(2)}) collective-permute-start(f32[3,4,256]{2,1,0:T(4,128)S(1)} %get-tuple-element.27), channel_id=1, source_target_pairs={{0,1},{1,2},{2,3},{4,5},{5,6},{6,7},{8,9},{9,10},{10,11},{12,13},{... | collective-permute-start | bytes 36872 | tf_op jit(solution)/shard_map/ppermute | solution.py:22
  95.1 7.2 %collective-permute-start.5 = (f32[3,24,4]{2,1,0:T(8,128)S(1)}, f32[3,24,4]{2,1,0:T(8,128)S(1)}, u32[]{:S(2)}, u32[]{:S(2)}) collective-permute-start(f32[3,24,4]{2,1,0:T(8,128)S(1)} %get-tuple-element.26), channel_id=1, source_target_pairs={{4,0},{8,4},{12,8},{5,1},{9,5},{13,9},{6,2},{10,6},{14,10},{7,3},{... | collective-permute-start | bytes 3464 | tf_op jit(solution)/shard_map/ppermute | solution.py:22
  96.4 6.7 %collective-permute-start.4 = (f32[3,24,4]{2,1,0:T(8,128)S(1)}, f32[3,24,4]{2,1,0:T(8,128)S(1)}, u32[]{:S(2)}, u32[]{:S(2)}) collective-permute-start(f32[3,24,4]{2,1,0:T(8,128)S(1)} %get-tuple-element.25), channel_id=1, source_target_pairs={{0,4},{4,8},{8,12},{1,5},{5,9},{9,13},{2,6},{6,10},{10,14},{3,7},{... | collective-permute-start | bytes 3464 | tf_op jit(solution)/shard_map/ppermute | solution.py:22
  136.7 28.0 %collective-permute-start.6 = (bf16[16,128,256]{2,1,0:T(8,128)(2,1)}, bf16[16,128,256]{2,1,0:T(8,128)(2,1)S(1)}, u32[]{:S(2)}, u32[]{:S(2)}) collective-permute-start(bf16[16,128,256]{2,1,0:T(8,128)(2,1)} %get-tuple-element.14), channel_id=1, source_target_pairs={{4,0},{8,4},{12,8},{5,1},{9,5},{13,9},{6,2},{10,6},{14,10},{7,3},{... | collective-permute-start | bytes 3145736 | tf_op jit(solution)/shard_map/ppermute | solution.py:22
  164.8 7.1 %copy-start.6 = (bf16[16,128,256]{2,1,0:T(8,128)(2,1)S(1)}, bf16[16,128,256]{2,1,0:T(8,128)(2,1)}, u32[]{:S(2)}) copy-start(bf16[16,128,256]{2,1,0:T(8,128)(2,1)} %get-tuple-element.11) | copy-start | bytes 3145732
  166.7 26.6 %collective-permute-start.7 = (bf16[16,128,256]{2,1,0:T(8,128)(2,1)S(1)}, bf16[16,128,256]{2,1,0:T(8,128)(2,1)S(1)}, u32[]{:S(2)}, u32[]{:S(2)}) collective-permute-start(bf16[16,128,256]{2,1,0:T(8,128)(2,1)S(1)} %add_convert_fusion.1), channel_id=1, source_target_pairs={{4,0},{8,4},{12,8},{5,1},{9,5},{13,9},{6,2},{10,6},{14,10},{7,3},{... | collective-permute-start | bytes 3145736 | tf_op jit(solution)/shard_map/ppermute | solution.py:22
  172.4 20.9 %copy-start.4 = (f32[16,128,256]{2,1,0:T(8,128)S(1)}, f32[16,128,256]{2,1,0:T(8,128)}, u32[]{:S(2)}) copy-start(f32[16,128,256]{2,1,0:T(8,128)} %get-tuple-element.12) | copy-start | bytes 6291460
  (3 other events, 5.4 us)
where the time goes:
time: 202 us; the launch traced here: 201 us
  waiting for transfers between devices  66.8 us (33%)
  Pallas kernels  52.2 us (26%)
  starting transfers between devices  32.4 us (16%)
  local copies, waits for them, and re-layouts  19.9 us (10%)
  other arithmetic  14.7 us (7%)
  blocking collectives  13 us (6%)
    ppermute x8, waiting for transfers between devices, from_behind(): lax.ppermute(value, axis, [(source, source + steps) for source in range(f...  65.4 us
    pallas_call x1, Pallas kernels, match(): pl.pallas_call(cost_kernel, grid=(rows,), in_specs=[pl.BlockSpec(memory_s...  22 us
    ppermute x8, starting transfers between devices, from_behind(): lax.ppermute(value, axis, [(source, source + steps) for source in range(f...  21.8 us
    pallas_call x1, Pallas kernels, match_grads(): pl.pallas_call(grad_kernel, grid=(rows,), in_specs=[pl.BlockSpec(memory_s...  20.5 us
    all_to_all x3, blocking collectives, to_rows(): return lax.all_to_all(array, 'ch', rows_dim, other_dim, tiled=True)  13 us
    all_to_all x3, starting transfers between devices, to_rows(): return lax.all_to_all(array, 'ch', rows_dim, other_dim, tiled=True)  10.6 us
    pallas_call x1, Pallas kernels, refine(): pl.pallas_call(functools.partial(refine_kernel, cols), out_shape=jax.Shap...  9.72 us
    all_to_all x6, local copies, waits for them, and re-layouts, to_rows(): return lax.all_to_all(array, 'ch', rows_dim, other_dim, tiled=True)  5.51 us
  transfers between devices with their start and end apart: 11, of which 6 were waited for; matrix products, arithmetic and copies ran while one was open for 12% of the time, Pallas kernels for 0%

commit v1 on v0

--- a/solution.py
+++ b/solution.py
@@ -12,6 +12,7 @@
 DISP = 256
 HALO = 4
 LANES = 128
+CHUNKS = 2
 VMEM = 56 * 1024 * 1024
 F32, BF16 = jnp.float32, jnp.bfloat16
 
@@ -89,7 +90,7 @@
 
 
 def grad_kernel(
-    offset_ref, left_ref, far_ref, mid_ref, near_ref, probs_ref, stats_ref, cots_ref,
+    base, offset_ref, left_ref, far_ref, mid_ref, near_ref, probs_ref, stats_ref, cots_ref,
     left_out, far_out, mid_out, near_out,
 ):
     row = pl.program_id(0)
@@ -103,8 +104,8 @@
 
     mean = column(stats_ref, row)
     spread = column(stats_ref, row + LANES // 2)
-    cot_mean = column(cots_ref, row)
-    cot_spread = column(cots_ref, row + LANES // 2)
+    cot_mean = column(cots_ref, row + base)
+    cot_spread = column(cots_ref, row + base + LANES // 2)
     probs = probs_ref[0]
     apart = levels_of(probs.shape) - mean
     grad_scores = probs * (cot_mean * apart + cot_spread * (apart * apart - spread))
@@ -221,43 +222,55 @@
     return out[:3, :cells].reshape(3, rows, cols)
 
 
-def row_block(array):
-    return pl.BlockSpec((1,) + array.shape[1:], lambda row: (row, 0, 0))
+def row_block(array, base=0):
+    return pl.BlockSpec((1,) + array.shape[1:], lambda row: (row + base, 0, 0))
 
 
 def whole_block(shape):
     return pl.BlockSpec(shape, lambda row: (0, 0))
 
 
-def match(offsets, left, window):
-    rows, _, tile = left.shape
+def cost_of(rows, tile):
+    return pl.CostEstimate(
+        flops=rows * tile * (3 * tile) * FEAT * 2,
+        bytes_accessed=rows * tile * DISP * 64,
+        transcendentals=rows * tile * DISP,
+    )
+
+
+def match(offsets, left, base, window):
+    tile = left.shape[2]
+    rows = window[0].shape[0]
     probs = jax.ShapeDtypeStruct((rows, tile, DISP), F32)
     stats = jax.ShapeDtypeStruct((tile, LANES), F32)
     return pl.pallas_call(
         cost_kernel,
         grid=(rows,),
-        in_specs=[pl.BlockSpec(memory_space=pltpu.SMEM), row_block(left)]
+        in_specs=[pl.BlockSpec(memory_space=pltpu.SMEM), row_block(left, base)]
         + [row_block(part) for part in window],
         out_specs=[row_block(probs), whole_block(stats.shape)],
         out_shape=[probs, stats],
         compiler_params=pltpu.CompilerParams(vmem_limit_bytes=VMEM),
+        cost_estimate=cost_of(rows, tile),
         name="match",
     )(offsets, left, *window)
 
 
-def match_grads(offsets, left, window, probs, stats, cots):
-    rows, feats, tile = left.shape
+def match_grads(offsets, left, base, window, probs, stats, cots):
+    feats, tile = left.shape[1:]
+    rows = window[0].shape[0]
     narrow = jax.ShapeDtypeStruct((rows, feats, tile), BF16)
     wide = jax.ShapeDtypeStruct((rows, feats, tile), F32)
     return pl.pallas_call(
-        grad_kernel,
+        functools.partial(grad_kernel, base),
         grid=(rows,),
-        in_specs=[pl.BlockSpec(memory_space=pltpu.SMEM), row_block(left)]
+        in_specs=[pl.BlockSpec(memory_space=pltpu.SMEM), row_block(left, base)]
         + [row_block(part) for part in window]
         + [row_block(probs), whole_block(stats.shape), whole_block(cots.shape)],
-        out_specs=[row_block(left)] * 4,
+        out_specs=[row_block(narrow)] * 4,
         out_shape=[narrow, narrow, wide, wide],
         compiler_params=pltpu.CompilerParams(vmem_limit_bytes=VMEM),
+        cost_estimate=cost_of(rows, tile),
         name="match_grads",
     )(offsets, left, *window, probs, stats, cots)
 
@@ -266,20 +279,33 @@
     return lax.all_to_all(array, "ch", rows_dim, other_dim, tiled=True)
 
 
+def chunk_count(rows):
+    return CHUNKS if rows % CHUNKS == 0 else 1
+
+
 def shards(left_feat, right_feat, offsets, valid, w_first, w_middle, w_last, grad_out):
-    near = to_rows(right_feat, 0, 1)
-    mid = from_behind(near, "col", 1)
+    whole_near = to_rows(right_feat, 0, 1)
+    left_feat, valid, grad_out, whole_near = lax.optimization_barrier(
+        (left_feat, valid, grad_out, whole_near)
+    )
+    rows, _, cols = whole_near.shape
+    chunks = chunk_count(rows)
+    step = rows // chunks
+    near = [whole_near[index * step : (index + 1) * step] for index in range(chunks)]
+    mid = [from_behind(part, "col", 1) for part in near]
     left = to_rows(left_feat, 0, 1)
     keep_cols = valid.astype(F32)
     planes = to_rows(jnp.stack([keep_cols, grad_out * keep_cols]), 1, 2)
     keep, grad_top = planes[0], planes[1]
-    far = from_behind(mid, "col", 1)
-    window = (far, mid, near)
-    probs, stats = match(offsets, left, window)
-    rows, cols = keep.shape
-    flipped = stats.T
-    coarse = offsets[0].astype(F32) / DISP + flipped[:rows]
-    spread = flipped[LANES // 2 : LANES // 2 + rows]
+    far = [from_behind(part, "col", 1) for part in mid]
+    windows = list(zip(far, mid, near))
+    matched = [
+        match(offsets, left, index * step, window) for index, window in enumerate(windows)
+    ]
+    flipped = [stats.T for _, stats in matched]
+    mean_level = jnp.concatenate([part[:step] for part in flipped])
+    spread = jnp.concatenate([part[LANES // 2 : LANES // 2 + step] for part in flipped])
+    coarse = offsets[0].astype(F32) / DISP + mean_level
     fields = jnp.stack([coarse * keep, spread * keep, grad_top])
     fields = with_halo(fields, ("row", "ch"), 1, HALO)
     fields = with_halo(fields, "col", 2, HALO)
@@ -295,17 +321,22 @@
     cots = jnp.concatenate(
         [grad_top + results[1] * keep, gap, results[2] * keep, gap]
     ).T
-    grad_left, far_grad, mid_grad, near_grad = match_grads(
-        offsets, left, window, probs, stats, cots
-    )
-    carried = from_behind(far_grad, "col", -1)
-    carried = from_behind((mid_grad + carried.astype(F32)).astype(BF16), "col", -1)
-    grad_right = (near_grad + carried.astype(F32)).astype(BF16)
-    return (
-        to_rows(refined, 1, 0),
-        to_rows(grad_left, 1, 0),
-        to_rows(grad_right, 1, 0),
-    )
+    left_parts, right_parts = [], []
+    for index, (window, (probs, stats)) in enumerate(zip(windows, matched)):
+        grad_left, far_grad, mid_grad, near_grad = match_grads(
+            offsets, left, index * step, window, probs, stats, cots
+        )
+        carried = from_behind(far_grad, "col", -1)
+        carried = from_behind((mid_grad + carried.astype(F32)).astype(BF16), "col", -1)
+        left_parts.append(to_rows(grad_left, 1, 0))
+        right_parts.append(to_rows((near_grad + carried.astype(F32)).astype(BF16), 1, 0))
+
+    def assemble(parts):
+        parts = [part.reshape((2, step) + part.shape[1:]) for part in parts]
+        stacked = jnp.stack(parts, axis=1)
+        return stacked.reshape((2 * rows,) + stacked.shape[3:])
+
+    return (to_rows(refined, 1, 0), assemble(left_parts), assemble(right_parts))
 
 
 def solution(mesh):

time: 202 us -> 188 us (0.931)
  waiting for transfers between devices: 66.8 us -> 37.9 us
  starting transfers between devices: 32.4 us -> 42.5 us
  blocking collectives: 13 us -> 21.9 us
  local copies, waits for them, and re-layouts: 19.9 us -> 14 us
  Pallas kernels: 52.2 us -> 56 us
  other arithmetic: 14.7 us -> 12.1 us
    ppermute x8 -> x12, waiting for transfers between devices: 65.4 us -> 37.9 us  [from_behind(): lax.ppermute(value, axis, [(source, source + steps) for source in range(f...]
    ppermute x8 -> x12, starting transfers between devices: 21.8 us -> 32.2 us  [from_behind(): lax.ppermute(value, axis, [(source, source + steps) for source in range(f...]
    all_to_all x3 -> x5, blocking collectives: 13 us -> 21.9 us  [to_rows(): return lax.all_to_all(array, 'ch', rows_dim, other_dim, tiled=True)]
    all_to_all x6 -> x3, local copies, waits for them, and re-layouts: 5.51 us -> 1.14 us  [to_rows(): return lax.all_to_all(array, 'ch', rows_dim, other_dim, tiled=True)]
    and x4, local copies, waits for them, and re-layouts: 5.43 us -> 1.56 us  [shards(): inside = (row_in[:, None] & col_in[None, :]).astype(F32)]
    another operation x2, local copies, waits for them, and re-layouts: 0.13 us -> 2.43 us  [assemble(): stacked = jnp.stack(parts, axis=1)]
    pallas_call x1 -> x2, Pallas kernels: 20.5 us -> 22.5 us  [match_grads(): pl.pallas_call(functools.partial(grad_kernel, base), grid=(rows,), in_spe...]
    pallas_call x1 -> x2, Pallas kernels: 22 us -> 23.8 us  [match(): pl.pallas_call(cost_kernel, grid=(rows,), in_specs=[pl.BlockSpec(memory_s...]
  transfers between devices with their start and end apart: 11 -> 15, of which waited for: 6 -> 7; matrix products, arithmetic and copies ran while one was open for 12% -> 10% of each run, Pallas kernels for 0% -> 12%
where the time goes in v1:
time: 188 us; the launch traced here: 186 us
  Pallas kernels  56 us (30%)
  starting transfers between devices  42.5 us (23%)
  waiting for transfers between devices  37.9 us (20%)
  blocking collectives  21.9 us (12%)
  local copies, waits for them, and re-layouts  14 us (7%)
  other arithmetic  12.1 us (6%)
    ppermute x12, waiting for transfers between devices, from_behind(): lax.ppermute(value, axis, [(source, source + steps) for source in range(f...  37.9 us
    ppermute x12, starting transfers between devices, from_behind(): lax.ppermute(value, axis, [(source, source + steps) for source in range(f...  32.2 us
    pallas_call x2, Pallas kernels, match(): pl.pallas_call(cost_kernel, grid=(rows,), in_specs=[pl.BlockSpec(memory_s...  23.8 us
    pallas_call x2, Pallas kernels, match_grads(): pl.pallas_call(functools.partial(grad_kernel, base), grid=(rows,), in_spe...  22.5 us
    all_to_all x5, blocking collectives, to_rows(): return lax.all_to_all(array, 'ch', rows_dim, other_dim, tiled=True)  21.9 us
    all_to_all x3, starting transfers between devices, to_rows(): return lax.all_to_all(array, 'ch', rows_dim, other_dim, tiled=True)  10.3 us
    pallas_call x1, Pallas kernels, refine(): pl.pallas_call(functools.partial(refine_kernel, cols), out_shape=jax.Shap...  9.72 us
    concatenate x4, other arithmetic, weight_side(): return jnp.concatenate([upper, upper, lower], axis=1)  4.4 us
  transfers between devices with their start and end apart: 15, of which 7 were waited for; matrix products, arithmetic and copies ran while one was open for 10% of the time, Pallas kernels for 12%

profile of v1, /device:TPU:0, one launch (start us, length us, event | category | flops | bytes accessed | tf_op | source)
XLA Modules:
  0.0 186.3 jit_solution(11589030382710466828)
XLA Ops:
  0.7 5.7 %all_to_all.127 = bf16[32,64,256]{2,1,0:T(8,128)(2,1)S(1)} all-to-all(bf16[32,64,256]{2,1,0:T(8,128)(2,1)} %param.9), channel_id=1, replica_groups=mesh['slab'=2,'col'=4,'row'=2,'ch'=2] {'ch'}, dimensions={0} | all-to-all | bytes 2097152 | tf_op jit(solution)/shard_map/all_to_all | solution.py:279
  7.2 3.3 %all-to-all-start.1 = ((f32[2,32,128]{2,0,1:T(2,128)}), f32[2,32,128]{2,0,1:T(2,128)S(1)}, u32[]{:S(2)}, u32[]{:S(2)}) async-start(f32[2,32,128]{2,0,1:T(2,128)} %pad_maximum_fusion.6), calls=%async_computation.1 | async-start | bytes 65536 | tf_op jit(solution)/shard_map/all_to_all | solution.py:279
  10.5 5.0 %collective-permute-start = (bf16[8,128,256]{2,1,0:T(8,128)(2,1)S(1)}, bf16[8,128,256]{2,1,0:T(8,128)(2,1)S(1)}, u32[]{:S(2)}, u32[]{:S(2)}) collective-permute-start(bf16[8,128,256]{2,1,0:T(8,128)(2,1)S(1)} %get-tuple-element.35.near_ref), channel_id=1, source_target_pairs={{0,4},{4,8},{8,12},{1,5},{5,9},{9,13},{2,6},{6,10},{10,14},{3,7},{... | collective-permute-start | bytes 1572872 | tf_op jit(solution)/shard_map/ppermute | solution.py:23
  15.5 3.5 %collective-permute-start.2 = (bf16[8,128,256]{2,1,0:T(8,128)(2,1)S(1)}, bf16[8,128,256]{2,1,0:T(8,128)(2,1)S(1)}, u32[]{:S(2)}, u32[]{:S(2)}) collective-permute-start(bf16[8,128,256]{2,1,0:T(8,128)(2,1)S(1)} %get-tuple-element.36.near_ref), channel_id=1, source_target_pairs={{0,4},{4,8},{8,12},{1,5},{5,9},{9,13},{2,6},{6,10},{10,14},{3,7},{... | collective-permute-start | bytes 1572872 | tf_op jit(solution)/shard_map/ppermute | solution.py:23
  24.5 3.6 %all-to-all-start.2 = ((bf16[32,64,256]{2,1,0:T(8,128)(2,1)}), bf16[32,64,256]{2,1,0:T(8,128)(2,1)S(1)}, u32[]{:S(2)}, u32[]{:S(2)}) async-start(bf16[32,64,256]{2,1,0:T(8,128)(2,1)} %param.8), calls=%async_computation.2 | async-start | bytes 2097152 | tf_op jit(solution)/shard_map/all_to_all | solution.py:279
  32.3 4.3 %collective-permute-start.1 = (bf16[8,128,256]{2,1,0:T(8,128)(2,1)S(1)}, bf16[8,128,256]{2,1,0:T(8,128)(2,1)}, u32[]{:S(2)}, u32[]{:S(2)}) collective-permute-start(bf16[8,128,256]{2,1,0:T(8,128)(2,1)S(1)} %collective-permute-done.mid_ref), channel_id=1, source_target_pairs={{0,4},{4,8},{8,12},{1,5},{5,9},{9,13},{2,6},{6,10},{10,14},{3,7},{... | collective-permute-start | bytes 1572872 | tf_op jit(solution)/shard_map/ppermute | solution.py:23
  36.6 2.4 %collective-permute-done.2.mid_ref = bf16[8,128,256]{2,1,0:T(8,128)(2,1)S(1)} collective-permute-done((bf16[8,128,256]{2,1,0:T(8,128)(2,1)S(1)}, bf16[8,128,256]{2,1,0:T(8,128)(2,1)S(1)}, u32[]{:S(2)}, u32[]{:S(2)}) %collective-permute-start.2) | collective-permute-done | bytes 524320 | tf_op jit(solution)/shard_map/ppermute | solution.py:23
  38.9 5.2 %collective-permute-start.3 = (bf16[8,128,256]{2,1,0:T(8,128)(2,1)S(1)}, bf16[8,128,256]{2,1,0:T(8,128)(2,1)}, u32[]{:S(2)}, u32[]{:S(2)}) collective-permute-start(bf16[8,128,256]{2,1,0:T(8,128)(2,1)S(1)} %collective-permute-done.2.mid_ref), channel_id=1, source_target_pairs={{0,4},{4,8},{8,12},{1,5},{5,9},{9,13},{2,6},{6,10},{10,14},{3,7},{... | collective-permute-start | bytes 1572872 | tf_op jit(solution)/shard_map/ppermute | solution.py:23
  49.0 12.0 %collective-permute-done.3.far_ref = bf16[8,128,256]{2,1,0:T(8,128)(2,1)} collective-permute-done((bf16[8,128,256]{2,1,0:T(8,128)(2,1)S(1)}, bf16[8,128,256]{2,1,0:T(8,128)(2,1)}, u32[]{:S(2)}, u32[]{:S(2)}) %collective-permute-start.3) | collective-permute-done | bytes 524320 | tf_op jit(solution)/shard_map/ppermute | solution.py:23
  61.0 11.9 %match.3 = (f32[8,256,256]{2,1,0:T(8,128)}, f32[256,128]{1,0:T(8,128)}) custom-call(s32[1]{0:T(128)S(6)} %copy.157.offset_ref, bf16[16,128,256]{2,1,0:T(8,128)(2,1)} %bitcast.93, bf16[8,128,256]{2,1,0:T(8,128)(2,1)} %collective-permute-done.3.far_ref, bf16[8,128,256]{2,1,0:T(8,128)(2,1)} %copy-done.3, bf16[8,128,256]{2,1,0:T(8,128)(2,1)} %copy-done.1), custom_call_target="tpu_custom_call" | custom-call | flops 402653184 | bytes 33554432 | tf_op jit(solution)/shard_map/match/pallas_call | solution.py:246
  73.0 11.9 %match.2 = (f32[8,256,256]{2,1,0:T(8,128)}, f32[256,128]{1,0:T(8,128)}) custom-call(s32[1]{0:T(128)S(6)} %copy.157.offset_ref, bf16[16,128,256]{2,1,0:T(8,128)(2,1)} %bitcast.94, bf16[8,128,256]{2,1,0:T(8,128)(2,1)} %collective-permute-done.1.far_ref, bf16[8,128,256]{2,1,0:T(8,128)(2,1)} %copy-done.2, bf16[8,128,256]{2,1,0:T(8,128)(2,1)} %copy-done), custom_call_target="tpu_custom_call" | custom-call | flops 402653184 | bytes 33554432 | tf_op jit(solution)/shard_map/match/pallas_call | solution.py:246
  89.2 3.2 %collective-permute-done.5 = f32[3,4,256]{2,1,0:T(4,128)S(1)} collective-permute-done((f32[3,4,256]{2,1,0:T(4,128)S(1)}, f32[3,4,256]{2,1,0:T(4,128)S(1)}, u32[]{:S(2)}, u32[]{:S(2)}) %collective-permute-start.5) | collective-permute-done | bytes 12320 | tf_op jit(solution)/shard_map/ppermute | solution.py:23
  92.5 4.5 %collective-permute-start.6 = (f32[3,24,4]{2,1,0:T(8,128)S(1)}, f32[3,24,4]{2,1,0:T(8,128)S(1)}, u32[]{:S(2)}, u32[]{:S(2)}) collective-permute-start(f32[3,24,4]{2,1,0:T(8,128)S(1)} %get-tuple-element.48), channel_id=1, source_target_pairs={{0,4},{4,8},{8,12},{1,5},{5,9},{9,13},{2,6},{6,10},{10,14},{3,7},{... | collective-permute-start | bytes 3464 | tf_op jit(solution)/shard_map/ppermute | solution.py:23
  99.4 3.5 %collective-permute-done.7 = f32[3,24,4]{2,1,0:T(8,128)S(1)} collective-permute-done((f32[3,24,4]{2,1,0:T(8,128)S(1)}, f32[3,24,4]{2,1,0:T(8,128)S(1)}, u32[]{:S(2)}, u32[]{:S(2)}) %collective-permute-start.7) | collective-permute-done | bytes 1184 | tf_op jit(solution)/shard_map/ppermute | solution.py:23
  103.9 9.7 %refine.1 = f32[8,6400]{1,0:T(8,128)} custom-call(f32[8,6400]{1,0:T(8,128)} %select_maximum_fusion.fields_ref, bf16[32,96]{1,0:T(8,128)(2,1)} %get-tuple-element.59.first_ref, bf16[288,96]{1,0:T(8,128)(2,1)} %get-tuple-element.57.middle_ref, bf16[16,96]{1,0:T(8,128)(2,1)} %pad_maximum_fusion.13.last_ref, bf16[32,96]{1,0:T(8,128)(2,1)} %get-tuple-element.60.last_back_ref, ...), custom_call_target="tpu_custom_call" | custom-call | tf_op jit(solution)/shard_map/refine/pallas_call | solution.py:208
  115.9 11.2 %match_grads.3 = (bf16[8,128,256]{2,1,0:T(8,128)(2,1)}, bf16[8,128,256]{2,1,0:T(8,128)(2,1)}, f32[8,128,256]{2,1,0:T(8,128)}, f32[8,128,256]{2,1,0:T(8,128)}) custom-call(s32[1]{0:T(128)S(6)} %copy.157.offset_ref, bf16[16,128,256]{2,1,0:T(8,128)(2,1)} %bitcast.95, bf16[8,128,256]{2,1,0:T(8,128)(2,1)} %collective-permute-done.3.far_ref, ...), custom_call_target="tpu_custom_call" | custom-call | flops 402653184 | bytes 33554432 | tf_op jit(solution)/shard_map/match_grads/pallas_call | solution.py:264
  128.4 11.3 %match_grads.2 = (bf16[8,128,256]{2,1,0:T(8,128)(2,1)}, bf16[8,128,256]{2,1,0:T(8,128)(2,1)}, f32[8,128,256]{2,1,0:T(8,128)}, f32[8,128,256]{2,1,0:T(8,128)}) custom-call(s32[1]{0:T(128)S(6)} %copy.157.offset_ref, bf16[16,128,256]{2,1,0:T(8,128)(2,1)} %bitcast.96, bf16[8,128,256]{2,1,0:T(8,128)(2,1)} %collective-permute-done.1.far_ref, ...), custom_call_target="tpu_custom_call" | custom-call | flops 402653184 | bytes 33554432 | tf_op jit(solution)/shard_map/match_grads/pallas_call | solution.py:264
  141.3 2.7 %collective-permute-done.10 = bf16[8,128,256]{2,1,0:T(8,128)(2,1)S(1)} collective-permute-done((bf16[8,128,256]{2,1,0:T(8,128)(2,1)}, bf16[8,128,256]{2,1,0:T(8,128)(2,1)S(1)}, u32[]{:S(2)}, u32[]{:S(2)}) %collective-permute-start.10) | collective-permute-done | bytes 524320 | tf_op jit(solution)/shard_map/ppermute | solution.py:23
  145.6 11.8 %collective-permute-done.8 = bf16[8,128,256]{2,1,0:T(8,128)(2,1)S(1)} collective-permute-done((bf16[8,128,256]{2,1,0:T(8,128)(2,1)}, bf16[8,128,256]{2,1,0:T(8,128)(2,1)S(1)}, u32[]{:S(2)}, u32[]{:S(2)}) %collective-permute-start.8) | collective-permute-done | bytes 524320 | tf_op jit(solution)/shard_map/ppermute | solution.py:23
  158.8 3.7 %all_to_all.128 = f32[16,2,128]{2,0,1:T(8,128)S(1)} all-to-all(f32[16,2,128]{2,0,1:T(8,128)S(1)} %fusion.5), channel_id=1, replica_groups=mesh['slab'=2,'col'=4,'row'=2,'ch'=2] {'ch'}, dimensions={1} | all-to-all | bytes 32768 | tf_op jit(solution)/shard_map/all_to_all | solution.py:279
  163.1 4.2 %all_to_all.129 = bf16[8,128,256]{2,0,1:T(8,128)(2,1)S(1)} all-to-all(bf16[8,128,256]{2,0,1:T(8,128)(2,1)S(1)} %copy.144), channel_id=1, replica_groups=mesh['slab'=2,'col'=4,'row'=2,'ch'=2] {'ch'}, dimensions={1} | all-to-all | bytes 1048576 | tf_op jit(solution)/shard_map/all_to_all | solution.py:279
  167.3 4.1 %all_to_all.130 = bf16[8,128,256]{2,0,1:T(8,128)(2,1)S(1)} all-to-all(bf16[8,128,256]{2,0,1:T(8,128)(2,1)S(1)} %copy.143), channel_id=1, replica_groups=mesh['slab'=2,'col'=4,'row'=2,'ch'=2] {'ch'}, dimensions={1} | all-to-all | bytes 1048576 | tf_op jit(solution)/shard_map/all_to_all | solution.py:279
  173.9 3.5 %all-to-all-start.7 = ((bf16[8,128,256]{2,0,1:T(8,128)(2,1)}), bf16[8,128,256]{2,0,1:T(8,128)(2,1)S(1)}, u32[]{:S(2)}, u32[]{:S(2)}) async-start(bf16[8,128,256]{2,0,1:T(8,128)(2,1)} %copy.147), calls=%async_computation.7 | async-start | bytes 1048576 | tf_op jit(solution)/shard_map/all_to_all | solution.py:279
  180.2 4.2 %all_to_all.131 = bf16[8,128,256]{2,0,1:T(8,128)(2,1)S(1)} all-to-all(bf16[8,128,256]{2,0,1:T(8,128)(2,1)S(1)} %copy.146), channel_id=1, replica_groups=mesh['slab'=2,'col'=4,'row'=2,'ch'=2] {'ch'}, dimensions={1} | all-to-all | bytes 1048576 | tf_op jit(solution)/shard_map/all_to_all | solution.py:279
  (143 shorter events, 38.3 us)
Async XLA Ops:
  7.2 17.3 %all-to-all-start.1 = ((f32[2,32,128]{2,0,1:T(2,128)}), f32[2,32,128]{2,0,1:T(2,128)S(1)}, u32[]{:S(2)}, u32[]{:S(2)}) async-start(f32[2,32,128]{2,0,1:T(2,128)} %pad_maximum_fusion.6), calls=%async_computation.1 | async-start | bytes 65536 | tf_op jit(solution)/shard_map/all_to_all | solution.py:279
  10.5 36.0 %copy-start = (bf16[8,128,256]{2,1,0:T(8,128)(2,1)}, bf16[8,128,256]{2,1,0:T(8,128)(2,1)S(1)}, u32[]{:S(2)}) copy-start(bf16[8,128,256]{2,1,0:T(8,128)(2,1)S(1)} %get-tuple-element.35.near_ref) | copy-start | bytes 1572868
  10.5 36.0 %copy-start.1 = (bf16[8,128,256]{2,1,0:T(8,128)(2,1)}, bf16[8,128,256]{2,1,0:T(8,128)(2,1)S(1)}, u32[]{:S(2)}) copy-start(bf16[8,128,256]{2,1,0:T(8,128)(2,1)S(1)} %get-tuple-element.36.near_ref) | copy-start | bytes 1572868
  10.5 21.8 %collective-permute-start = (bf16[8,128,256]{2,1,0:T(8,128)(2,1)S(1)}, bf16[8,128,256]{2,1,0:T(8,128)(2,1)S(1)}, u32[]{:S(2)}, u32[]{:S(2)}) collective-permute-start(bf16[8,128,256]{2,1,0:T(8,128)(2,1)S(1)} %get-tuple-element.35.near_ref), channel_id=1, source_target_pairs={{0,4},{4,8},{8,12},{1,5},{5,9},{9,13},{2,6},{6,10},{10,14},{3,7},{... | collective-permute-start | bytes 1572872 | tf_op jit(solution)/shard_map/ppermute | solution.py:23
  15.5 23.4 %collective-permute-start.2 = (bf16[8,128,256]{2,1,0:T(8,128)(2,1)S(1)}, bf16[8,128,256]{2,1,0:T(8,128)(2,1)S(1)}, u32[]{:S(2)}, u32[]{:S(2)}) collective-permute-start(bf16[8,128,256]{2,1,0:T(8,128)(2,1)S(1)} %get-tuple-element.36.near_ref), channel_id=1, source_target_pairs={{0,4},{4,8},{8,12},{1,5},{5,9},{9,13},{2,6},{6,10},{10,14},{3,7},{... | collective-permute-start | bytes 1572872 | tf_op jit(solution)/shard_map/ppermute | solution.py:23
  24.5 21.0 %all-to-all-start.2 = ((bf16[32,64,256]{2,1,0:T(8,128)(2,1)}), bf16[32,64,256]{2,1,0:T(8,128)(2,1)S(1)}, u32[]{:S(2)}, u32[]{:S(2)}) async-start(bf16[32,64,256]{2,1,0:T(8,128)(2,1)} %param.8), calls=%async_computation.2 | async-start | bytes 2097152 | tf_op jit(solution)/shard_map/all_to_all | solution.py:279
  32.3 40.6 %copy-start.2 = (bf16[8,128,256]{2,1,0:T(8,128)(2,1)}, bf16[8,128,256]{2,1,0:T(8,128)(2,1)S(1)}, u32[]{:S(2)}) copy-start(bf16[8,128,256]{2,1,0:T(8,128)(2,1)S(1)} %collective-permute-done.mid_ref) | copy-start | bytes 1572868
  32.3 40.6 %collective-permute-start.1 = (bf16[8,128,256]{2,1,0:T(8,128)(2,1)S(1)}, bf16[8,128,256]{2,1,0:T(8,128)(2,1)}, u32[]{:S(2)}, u32[]{:S(2)}) collective-permute-start(bf16[8,128,256]{2,1,0:T(8,128)(2,1)S(1)} %collective-permute-done.mid_ref), channel_id=1, source_target_pairs={{0,4},{4,8},{8,12},{1,5},{5,9},{9,13},{2,6},{6,10},{10,14},{3,7},{... | collective-permute-start | bytes 1572872 | tf_op jit(solution)/shard_map/ppermute | solution.py:23
  38.9 22.1 %copy-start.3 = (bf16[8,128,256]{2,1,0:T(8,128)(2,1)}, bf16[8,128,256]{2,1,0:T(8,128)(2,1)S(1)}, u32[]{:S(2)}) copy-start(bf16[8,128,256]{2,1,0:T(8,128)(2,1)S(1)} %collective-permute-done.2.mid_ref) | copy-start | bytes 1572868
  38.9 22.1 %collective-permute-start.3 = (bf16[8,128,256]{2,1,0:T(8,128)(2,1)S(1)}, bf16[8,128,256]{2,1,0:T(8,128)(2,1)}, u32[]{:S(2)}, u32[]{:S(2)}) collective-permute-start(bf16[8,128,256]{2,1,0:T(8,128)(2,1)S(1)} %collective-permute-done.2.mid_ref), channel_id=1, source_target_pairs={{0,4},{4,8},{8,12},{1,5},{5,9},{9,13},{2,6},{6,10},{10,14},{3,7},{... | collective-permute-start | bytes 1572872 | tf_op jit(solution)/shard_map/ppermute | solution.py:23
  72.9 25.6 %copy-start.21 = (bf16[16,32]{1,0:T(8,128)(2,1)S(1)}, bf16[16,32]{1,0:T(8,128)(2,1)}, u32[]{:S(2)}) copy-start(bf16[16,32]{1,0:T(8,128)(2,1)} %subtract_convert_fusion.2) | copy-start | bytes 3076
  72.9 26.3 %copy-start.16 = (f32[1,16,2,128]{3,1,2,0:T(8,128)S(1)}, f32[1,16,2,128]{3,1,2,0:T(8,128)}, u32[]{:S(2)}) copy-start(f32[1,16,2,128]{3,1,2,0:T(8,128)} %get-tuple-element.53) | copy-start | bytes 49156
  72.9 26.3 %copy-start.14 = (f32[1,16,2,128]{3,1,2,0:T(8,128)S(1)}, f32[1,16,2,128]{3,1,2,0:T(8,128)}, u32[]{:S(2)}) copy-start(f32[1,16,2,128]{3,1,2,0:T(8,128)} %get-tuple-element.52) | copy-start | bytes 49156
  86.3 2.9 %collective-permute-start.4 = (f32[3,4,256]{2,1,0:T(4,128)S(1)}, f32[3,4,256]{2,1,0:T(4,128)S(1)}, u32[]{:S(2)}, u32[]{:S(2)}) collective-permute-start(f32[3,4,256]{2,1,0:T(4,128)S(1)} %get-tuple-element.50), channel_id=1, source_target_pairs={{0,1},{1,2},{2,3},{4,5},{5,6},{6,7},{8,9},{9,10},{10,11},{12,13},{... | collective-permute-start | bytes 36872 | tf_op jit(solution)/shard_map/ppermute | solution.py:23
  87.9 4.5 %collective-permute-start.5 = (f32[3,4,256]{2,1,0:T(4,128)S(1)}, f32[3,4,256]{2,1,0:T(4,128)S(1)}, u32[]{:S(2)}, u32[]{:S(2)}) collective-permute-start(f32[3,4,256]{2,1,0:T(4,128)S(1)} %get-tuple-element.51), channel_id=1, source_target_pairs={{1,0},{2,1},{3,2},{5,4},{6,5},{7,6},{9,8},{10,9},{11,10},{13,12},{... | collective-permute-start | bytes 36872 | tf_op jit(solution)/shard_map/ppermute | solution.py:23
  92.5 6.9 %collective-permute-start.6 = (f32[3,24,4]{2,1,0:T(8,128)S(1)}, f32[3,24,4]{2,1,0:T(8,128)S(1)}, u32[]{:S(2)}, u32[]{:S(2)}) collective-permute-start(f32[3,24,4]{2,1,0:T(8,128)S(1)} %get-tuple-element.48), channel_id=1, source_target_pairs={{0,4},{4,8},{8,12},{1,5},{5,9},{9,13},{2,6},{6,10},{10,14},{3,7},{... | collective-permute-start | bytes 3464 | tf_op jit(solution)/shard_map/ppermute | solution.py:23
  97.0 5.9 %collective-permute-start.7 = (f32[3,24,4]{2,1,0:T(8,128)S(1)}, f32[3,24,4]{2,1,0:T(8,128)S(1)}, u32[]{:S(2)}, u32[]{:S(2)}) collective-permute-start(f32[3,24,4]{2,1,0:T(8,128)S(1)} %get-tuple-element.49), channel_id=1, source_target_pairs={{4,0},{8,4},{12,8},{5,1},{9,5},{13,9},{6,2},{10,6},{14,10},{7,3},{... | collective-permute-start | bytes 3464 | tf_op jit(solution)/shard_map/ppermute | solution.py:23
  127.1 16.9 %collective-permute-start.10 = (bf16[8,128,256]{2,1,0:T(8,128)(2,1)}, bf16[8,128,256]{2,1,0:T(8,128)(2,1)S(1)}, u32[]{:S(2)}, u32[]{:S(2)}) collective-permute-start(bf16[8,128,256]{2,1,0:T(8,128)(2,1)} %get-tuple-element.34), channel_id=1, source_target_pairs={{4,0},{8,4},{12,8},{5,1},{9,5},{13,9},{6,2},{10,6},{14,10},{7,3},{... | collective-permute-start | bytes 1572872 | tf_op jit(solution)/shard_map/ppermute | solution.py:23
  139.7 17.6 %collective-permute-start.8 = (bf16[8,128,256]{2,1,0:T(8,128)(2,1)}, bf16[8,128,256]{2,1,0:T(8,128)(2,1)S(1)}, u32[]{:S(2)}, u32[]{:S(2)}) collective-permute-start(bf16[8,128,256]{2,1,0:T(8,128)(2,1)} %get-tuple-element.31), channel_id=1, source_target_pairs={{4,0},{8,4},{12,8},{5,1},{9,5},{13,9},{6,2},{10,6},{14,10},{7,3},{... | collective-permute-start | bytes 1572872 | tf_op jit(solution)/shard_map/ppermute | solution.py:23
  144.0 18.5 %copy-start.11 = (bf16[8,128,256]{2,1,0:T(8,128)(2,1)S(1)}, bf16[8,128,256]{2,1,0:T(8,128)(2,1)}, u32[]{:S(2)}) copy-start(bf16[8,128,256]{2,1,0:T(8,128)(2,1)} %get-tuple-element.26) | copy-start | bytes 1572868
  144.1 18.7 %copy-start.10 = (bf16[8,128,256]{2,1,0:T(8,128)(2,1)S(1)}, bf16[8,128,256]{2,1,0:T(8,128)(2,1)}, u32[]{:S(2)}) copy-start(bf16[8,128,256]{2,1,0:T(8,128)(2,1)} %get-tuple-element.28) | copy-start | bytes 1572868
  144.1 28.6 %collective-permute-start.11 = (bf16[8,128,256]{2,1,0:T(8,128)(2,1)S(1)}, bf16[8,128,256]{2,1,0:T(8,128)(2,1)S(1)}, u32[]{:S(2)}, u32[]{:S(2)}) collective-permute-start(bf16[8,128,256]{2,1,0:T(8,128)(2,1)S(1)} %add_convert_fusion.1), channel_id=1, source_target_pairs={{4,0},{8,4},{12,8},{5,1},{9,5},{13,9},{6,2},{10,6},{14,10},{7,3},{... | collective-permute-start | bytes 1572872 | tf_op jit(solution)/shard_map/ppermute | solution.py:23
  157.4 22.3 %collective-permute-start.9 = (bf16[8,128,256]{2,1,0:T(8,128)(2,1)S(1)}, bf16[8,128,256]{2,1,0:T(8,128)(2,1)S(1)}, u32[]{:S(2)}, u32[]{:S(2)}) collective-permute-start(bf16[8,128,256]{2,1,0:T(8,128)(2,1)S(1)} %add_convert_fusion.3), channel_id=1, source_target_pairs={{4,0},{8,4},{12,8},{5,1},{9,5},{13,9},{6,2},{10,6},{14,10},{7,3},{... | collective-permute-start | bytes 1572872 | tf_op jit(solution)/shard_map/ppermute | solution.py:23
  173.9 6.3 %all-to-all-start.7 = ((bf16[8,128,256]{2,0,1:T(8,128)(2,1)}), bf16[8,128,256]{2,0,1:T(8,128)(2,1)S(1)}, u32[]{:S(2)}, u32[]{:S(2)}) async-start(bf16[8,128,256]{2,0,1:T(8,128)(2,1)} %copy.147), calls=%async_computation.7 | async-start | bytes 1048576 | tf_op jit(solution)/shard_map/all_to_all | solution.py:279
  (14 other events, 146.5 us)

commit v2 on v1

--- a/solution.py
+++ b/solution.py
@@ -247,7 +247,8 @@
         cost_kernel,
         grid=(rows,),
         in_specs=[pl.BlockSpec(memory_space=pltpu.SMEM), row_block(left, base)]
-        + [row_block(part) for part in window],
+        + [row_block(part) for part in window[:2]]
+        + [row_block(window[2], base)],
         out_specs=[row_block(probs), whole_block(stats.shape)],
         out_shape=[probs, stats],
         compiler_params=pltpu.CompilerParams(vmem_limit_bytes=VMEM),
@@ -265,7 +266,8 @@
         functools.partial(grad_kernel, base),
         grid=(rows,),
         in_specs=[pl.BlockSpec(memory_space=pltpu.SMEM), row_block(left, base)]
-        + [row_block(part) for part in window]
+        + [row_block(part) for part in window[:2]]
+        + [row_block(window[2], base)]
         + [row_block(probs), whole_block(stats.shape), whole_block(cots.shape)],
         out_specs=[row_block(narrow)] * 4,
         out_shape=[narrow, narrow, wide, wide],
@@ -284,21 +286,31 @@
 
 
 def shards(left_feat, right_feat, offsets, valid, w_first, w_middle, w_last, grad_out):
-    whole_near = to_rows(right_feat, 0, 1)
-    left_feat, valid, grad_out, whole_near = lax.optimization_barrier(
-        (left_feat, valid, grad_out, whole_near)
-    )
-    rows, _, cols = whole_near.shape
+    double_rows, chans, cols = right_feat.shape
+    rows = double_rows // 2
     chunks = chunk_count(rows)
     step = rows // chunks
-    near = [whole_near[index * step : (index + 1) * step] for index in range(chunks)]
-    mid = [from_behind(part, "col", 1) for part in near]
+    halves = right_feat.reshape(2, chunks, step, chans, cols)
+    raw_mid = [
+        from_behind(halves[:, index].reshape(2 * step, chans, cols), "col", 1)
+        for index in range(chunks - 1)
+    ]
+    near = to_rows(right_feat, 0, 1)
+    left_feat, valid, grad_out, near = lax.optimization_barrier(
+        (left_feat, valid, grad_out, near)
+    )
+    last_near = near[rows - step :]
+    if raw_mid:
+        raw_mid, last_near = lax.optimization_barrier((raw_mid, last_near))
+    raw_far = [from_behind(part, "col", 1) for part in raw_mid]
+    last_mid = from_behind(last_near, "col", 1)
+    mid = [to_rows(part, 0, 1) for part in raw_mid] + [last_mid]
     left = to_rows(left_feat, 0, 1)
     keep_cols = valid.astype(F32)
     planes = to_rows(jnp.stack([keep_cols, grad_out * keep_cols]), 1, 2)
     keep, grad_top = planes[0], planes[1]
-    far = [from_behind(part, "col", 1) for part in mid]
-    windows = list(zip(far, mid, near))
+    far = [to_rows(part, 0, 1) for part in raw_far] + [from_behind(last_mid, "col", 1)]
+    windows = [(far_part, mid_part, near) for far_part, mid_part in zip(far, mid)]
     matched = [
         match(offsets, left, index * step, window) for index, window in enumerate(windows)
     ]
@@ -326,17 +338,20 @@
         grad_left, far_grad, mid_grad, near_grad = match_grads(
             offsets, left, index * step, window, probs, stats, cots
         )
+        left_parts.append(grad_left)
+        swap = index == chunks - 1
+        if swap:
+            far_grad, mid_grad, near_grad = (
+                to_rows(part, 1, 0) for part in (far_grad, mid_grad, near_grad)
+            )
         carried = from_behind(far_grad, "col", -1)
         carried = from_behind((mid_grad + carried.astype(F32)).astype(BF16), "col", -1)
-        left_parts.append(to_rows(grad_left, 1, 0))
-        right_parts.append(to_rows((near_grad + carried.astype(F32)).astype(BF16), 1, 0))
-
-    def assemble(parts):
-        parts = [part.reshape((2, step) + part.shape[1:]) for part in parts]
-        stacked = jnp.stack(parts, axis=1)
-        return stacked.reshape((2 * rows,) + stacked.shape[3:])
-
-    return (to_rows(refined, 1, 0), assemble(left_parts), assemble(right_parts))
+        total = (near_grad + carried.astype(F32)).astype(BF16)
+        total = total if swap else to_rows(total, 1, 0)
+        right_parts.append(total.reshape(2, step, chans, cols))
+    grad_right = jnp.stack(right_parts, axis=1).reshape(double_rows, chans, cols)
+    grad_left = to_rows(jnp.concatenate(left_parts), 1, 0)
+    return (to_rows(refined, 1, 0), grad_left, grad_right)
 
 
 def solution(mesh):

time: 188 us -> 193 us (1.027)
  blocking collectives: 21.9 us -> 41 us
  waiting for transfers between devices: 37.9 us -> 22 us
  starting transfers between devices: 42.5 us -> 37.7 us
  local copies, waits for them, and re-layouts: 14 us -> 18.4 us
    all_to_all x5 -> x9, blocking collectives: 21.9 us -> 41 us  [to_rows(): return lax.all_to_all(array, 'ch', rows_dim, other_dim, tiled=True)]
    ppermute x12, waiting for transfers between devices: 37.9 us -> 22 us  [from_behind(): lax.ppermute(value, axis, [(source, source + steps) for source in range(f...]
    all_to_all x3 -> x10, local copies, waits for them, and re-layouts: 1.14 us -> 5.8 us  [to_rows(): return lax.all_to_all(array, 'ch', rows_dim, other_dim, tiled=True)]
    all_to_all x3 -> x2, starting transfers between devices: 10.3 us -> 6.85 us  [to_rows(): return lax.all_to_all(array, 'ch', rows_dim, other_dim, tiled=True)]
    pallas_call x2 -> x3, local copies, waits for them, and re-layouts: 0.59 us -> 2.65 us  [match_grads(): pl.pallas_call(functools.partial(grad_kernel, base), grid=(rows,), in_spe...]
  transfers between devices with their start and end apart: 15 -> 14, of which waited for: 7 -> 5; matrix products, arithmetic and copies ran while one was open for 10% -> 12% of each run, Pallas kernels for 12% -> 12%
where the time goes in v2:
time: 193 us; the launch traced here: 190 us
  Pallas kernels  56 us (29%)
  blocking collectives  41 us (21%)
  starting transfers between devices  37.7 us (20%)
  waiting for transfers between devices  22 us (11%)
  local copies, waits for them, and re-layouts  18.4 us (10%)
  other arithmetic  13.1 us (7%)
  between operations  2.01 us (1%)
    all_to_all x9, blocking collectives, to_rows(): return lax.all_to_all(array, 'ch', rows_dim, other_dim, tiled=True)  41 us
    ppermute x12, starting transfers between devices, from_behind(): lax.ppermute(value, axis, [(source, source + steps) for source in range(f...  30.8 us
    pallas_call x2, Pallas kernels, match(): pl.pallas_call(cost_kernel, grid=(rows,), in_specs=[pl.BlockSpec(memory_s...  23.8 us
    pallas_call x2, Pallas kernels, match_grads(): pl.pallas_call(functools.partial(grad_kernel, base), grid=(rows,), in_spe...  22.5 us
    ppermute x12, waiting for transfers between devices, from_behind(): lax.ppermute(value, axis, [(source, source + steps) for source in range(f...  22 us
    pallas_call x1, Pallas kernels, refine(): pl.pallas_call(functools.partial(refine_kernel, cols), out_shape=jax.Shap...  9.7 us
    all_to_all x2, starting transfers between devices, to_rows(): return lax.all_to_all(array, 'ch', rows_dim, other_dim, tiled=True)  6.85 us
    all_to_all x10, local copies, waits for them, and re-layouts, to_rows(): return lax.all_to_all(array, 'ch', rows_dim, other_dim, tiled=True)  5.8 us
  transfers between devices with their start and end apart: 14, of which 5 were waited for; matrix products, arithmetic and copies ran while one was open for 12% of the time, Pallas kernels for 12%

profile of v2, /device:TPU:0, one launch (start us, length us, event | category | flops | bytes accessed | tf_op | source)
XLA Modules:
  0.0 190.2 jit_solution(10341054282789176185)
XLA Ops:
  0.7 5.8 %all_to_all.190 = bf16[32,64,256]{2,1,0:T(8,128)(2,1)S(1)} all-to-all(bf16[32,64,256]{2,1,0:T(8,128)(2,1)} %param.9), channel_id=1, replica_groups=mesh['slab'=2,'col'=4,'row'=2,'ch'=2] {'ch'}, dimensions={0} | all-to-all | bytes 2097152 | tf_op jit(solution)/shard_map/all_to_all | solution.py:281
  7.3 3.3 %all-to-all-start.1 = ((f32[2,32,128]{2,0,1:T(2,128)}), f32[2,32,128]{2,0,1:T(2,128)S(1)}, u32[]{:S(2)}, u32[]{:S(2)}) async-start(f32[2,32,128]{2,0,1:T(2,128)} %pad_maximum_fusion.6), calls=%async_computation.1 | async-start | bytes 65536 | tf_op jit(solution)/shard_map/all_to_all | solution.py:281
  10.6 5.0 %collective-permute-start = (bf16[16,64,256]{2,1,0:T(8,128)(2,1)S(1)}, bf16[16,64,256]{2,1,0:T(8,128)(2,1)S(1)}, u32[]{:S(2)}, u32[]{:S(2)}) collective-permute-start(bf16[16,64,256]{2,1,0:T(8,128)(2,1)S(1)} %bitcast.143), channel_id=1, source_target_pairs={{0,4},{4,8},{8,12},{1,5},{5,9},{9,13},{2,6},{6,10},{10,14},{3,7},{... | collective-permute-start | bytes 1572872 | tf_op jit(solution)/shard_map/ppermute | solution.py:23
  19.2 3.6 %all-to-all-start.2 = ((bf16[32,64,256]{2,1,0:T(8,128)(2,1)}), bf16[32,64,256]{2,1,0:T(8,128)(2,1)S(1)}, u32[]{:S(2)}, u32[]{:S(2)}) async-start(bf16[32,64,256]{2,1,0:T(8,128)(2,1)} %param.8), calls=%async_computation.2 | async-start | bytes 2097152 | tf_op jit(solution)/shard_map/all_to_all | solution.py:281
  27.4 4.4 %collective-permute-start.2 = (bf16[8,128,256]{2,1,0:T(8,128)(2,1)S(1)}, bf16[8,128,256]{2,1,0:T(8,128)(2,1)S(1)}, u32[]{:S(2)}, u32[]{:S(2)}) collective-permute-start(bf16[8,128,256]{2,1,0:T(8,128)(2,1)S(1)} %slice.58), channel_id=1, source_target_pairs={{0,4},{4,8},{8,12},{1,5},{5,9},{9,13},{2,6},{6,10},{10,14},{3,7},{... | collective-permute-start | bytes 1572872 | tf_op jit(solution)/shard_map/ppermute | solution.py:23
  34.5 3.5 %collective-permute-start.1 = (bf16[16,64,256]{2,1,0:T(8,128)(2,1)S(1)}, bf16[16,64,256]{2,1,0:T(8,128)(2,1)S(1)}, u32[]{:S(2)}, u32[]{:S(2)}) collective-permute-start(bf16[16,64,256]{2,1,0:T(8,128)(2,1)S(1)} %collective-permute-done), channel_id=1, source_target_pairs={{0,4},{4,8},{8,12},{1,5},{5,9},{9,13},{2,6},{6,10},{10,14},{3,7},{... | collective-permute-start | bytes 1572872 | tf_op jit(solution)/shard_map/ppermute | solution.py:23
  38.0 6.1 %collective-permute-done.2.mid_ref = bf16[8,128,256]{2,1,0:T(8,128)(2,1)S(1)} collective-permute-done((bf16[8,128,256]{2,1,0:T(8,128)(2,1)S(1)}, bf16[8,128,256]{2,1,0:T(8,128)(2,1)S(1)}, u32[]{:S(2)}, u32[]{:S(2)}) %collective-permute-start.2) | collective-permute-done | bytes 524320 | tf_op jit(solution)/shard_map/ppermute | solution.py:23
  44.1 4.4 %collective-permute-start.3 = (bf16[8,128,256]{2,1,0:T(8,128)(2,1)S(1)}, bf16[8,128,256]{2,1,0:T(8,128)(2,1)S(1)}, u32[]{:S(2)}, u32[]{:S(2)}) collective-permute-start(bf16[8,128,256]{2,1,0:T(8,128)(2,1)S(1)} %collective-permute-done.2.mid_ref), channel_id=1, source_target_pairs={{0,4},{4,8},{8,12},{1,5},{5,9},{9,13},{2,6},{6,10},{10,14},{3,7},{... | collective-permute-start | bytes 1572872 | tf_op jit(solution)/shard_map/ppermute | solution.py:23
  54.2 4.1 %all_to_all.191 = bf16[16,64,256]{2,1,0:T(8,128)(2,1)S(1)} all-to-all(bf16[16,64,256]{2,1,0:T(8,128)(2,1)S(1)} %collective-permute-done), channel_id=1, replica_groups=mesh['slab'=2,'col'=4,'row'=2,'ch'=2] {'ch'}, dimensions={0} | all-to-all | bytes 1048576 | tf_op jit(solution)/shard_map/all_to_all | solution.py:281
  59.2 4.1 %all_to_all.192 = bf16[16,64,256]{2,1,0:T(8,128)(2,1)S(1)} all-to-all(bf16[16,64,256]{2,1,0:T(8,128)(2,1)S(1)} %collective-permute-done.1), channel_id=1, replica_groups=mesh['slab'=2,'col'=4,'row'=2,'ch'=2] {'ch'}, dimensions={0} | all-to-all | bytes 1048576 | tf_op jit(solution)/shard_map/all_to_all | solution.py:281
  64.3 11.8 %match.2 = (f32[8,256,256]{2,1,0:T(8,128)}, f32[256,128]{1,0:T(8,128)}) custom-call(s32[1]{0:T(128)S(6)} %copy.229.offset_ref, bf16[16,128,256]{2,1,0:T(8,128)(2,1)} %bitcast.117, bf16[8,128,256]{2,1,0:T(8,128)(2,1)} %bitcast.123, bf16[8,128,256]{2,1,0:T(8,128)(2,1)} %bitcast.121, bf16[16,128,256]{2,1,0:T(8,128)(2,1)} %bitcast.113), custom_call_target="tpu_custom_call" | custom-call | flops 402653184 | bytes 33554432 | tf_op jit(solution)/shard_map/match/pallas_call | solution.py:246
  76.9 12.0 %match.3 = (f32[8,256,256]{2,1,0:T(8,128)}, f32[256,128]{1,0:T(8,128)}) custom-call(s32[1]{0:T(128)S(6)} %copy.229.offset_ref, bf16[16,128,256]{2,1,0:T(8,128)(2,1)} %bitcast.118, bf16[8,128,256]{2,1,0:T(8,128)(2,1)} %copy-done.3, bf16[8,128,256]{2,1,0:T(8,128)(2,1)} %copy-done.2, bf16[16,128,256]{2,1,0:T(8,128)(2,1)} %bitcast.114), custom_call_target="tpu_custom_call" | custom-call | flops 402653184 | bytes 33554432 | tf_op jit(solution)/shard_map/match/pallas_call | solution.py:246
  96.6 3.5 %collective-permute-start.6 = (f32[3,24,4]{2,1,0:T(8,128)S(1)}, f32[3,24,4]{2,1,0:T(8,128)S(1)}, u32[]{:S(2)}, u32[]{:S(2)}) collective-permute-start(f32[3,24,4]{2,1,0:T(8,128)S(1)} %get-tuple-element.50), channel_id=1, source_target_pairs={{0,4},{4,8},{8,12},{1,5},{5,9},{9,13},{2,6},{6,10},{10,14},{3,7},{... | collective-permute-start | bytes 3464 | tf_op jit(solution)/shard_map/ppermute | solution.py:23
  102.4 3.5 %collective-permute-done.7 = f32[3,24,4]{2,1,0:T(8,128)S(1)} collective-permute-done((f32[3,24,4]{2,1,0:T(8,128)S(1)}, f32[3,24,4]{2,1,0:T(8,128)S(1)}, u32[]{:S(2)}, u32[]{:S(2)}) %collective-permute-start.7) | collective-permute-done | bytes 1184 | tf_op jit(solution)/shard_map/ppermute | solution.py:23
  106.9 9.7 %refine.1 = f32[8,6400]{1,0:T(8,128)} custom-call(f32[8,6400]{1,0:T(8,128)} %select_maximum_fusion.fields_ref, bf16[32,96]{1,0:T(8,128)(2,1)} %get-tuple-element.61.first_ref, bf16[288,96]{1,0:T(8,128)(2,1)} %get-tuple-element.59.middle_ref, bf16[16,96]{1,0:T(8,128)(2,1)} %pad_maximum_fusion.13.last_ref, bf16[32,96]{1,0:T(8,128)(2,1)} %get-tuple-element.62.last_back_ref, ...), custom_call_target="tpu_custom_call" | custom-call | tf_op jit(solution)/shard_map/refine/pallas_call | solution.py:208
  118.9 11.2 %match_grads.2 = (bf16[8,128,256]{2,1,0:T(8,128)(2,1)}, bf16[8,128,256]{2,1,0:T(8,128)(2,1)}, f32[8,128,256]{2,1,0:T(8,128)}, f32[8,128,256]{2,1,0:T(8,128)}) custom-call(s32[1]{0:T(128)S(6)} %copy.229.offset_ref, bf16[16,128,256]{2,1,0:T(8,128)(2,1)} %bitcast.119, bf16[8,128,256]{2,1,0:T(8,128)(2,1)} %bitcast.124, bf16[8,128,256]{2,1,0:T(8,128)(2,1)} %bitcast.122, ...), custom_call_target="tpu_custom_call" | custom-call | flops 402653184 | bytes 33554432 | tf_op jit(solution)/shard_map/match_grads/pallas_call | solution.py:265
  131.4 11.3 %match_grads.3 = (bf16[8,128,256]{2,1,0:T(8,128)(2,1)}, bf16[8,128,256]{2,1,0:T(8,128)(2,1)}, f32[8,128,256]{2,1,0:T(8,128)}, f32[8,128,256]{2,1,0:T(8,128)}) custom-call(s32[1]{0:T(128)S(6)} %copy.229.offset_ref, bf16[16,128,256]{2,1,0:T(8,128)(2,1)} %bitcast.120, bf16[8,128,256]{2,1,0:T(8,128)(2,1)} %copy-done.3, bf16[8,128,256]{2,1,0:T(8,128)(2,1)} %copy-done.2, ...), custom_call_target="tpu_custom_call" | custom-call | flops 402653184 | bytes 33554432 | tf_op jit(solution)/shard_map/match_grads/pallas_call | solution.py:265
  144.2 4.7 %all_to_all.193 = bf16[8,128,256]{2,0,1:T(8,128)(2,1)S(1)} all-to-all(bf16[8,128,256]{2,0,1:T(8,128)(2,1)S(1)} %copy.210), channel_id=1, replica_groups=mesh['slab'=2,'col'=4,'row'=2,'ch'=2] {'ch'}, dimensions={1} | all-to-all | bytes 1048576 | tf_op jit(solution)/shard_map/all_to_all | solution.py:281
  151.0 4.9 %all_to_all.194 = f32[8,128,256]{2,0,1:T(8,128)S(1)} all-to-all(f32[8,128,256]{2,0,1:T(8,128)S(1)} %copy.207), channel_id=1, replica_groups=mesh['slab'=2,'col'=4,'row'=2,'ch'=2] {'ch'}, dimensions={1} | all-to-all | bytes 2097152 | tf_op jit(solution)/shard_map/all_to_all | solution.py:281
  157.9 8.0 %collective-permute-done.10 = bf16[16,64,256]{2,1,0:T(8,128)(2,1)S(1)} collective-permute-done((bf16[16,64,256]{2,1,0:T(8,128)(2,1)S(1)}, bf16[16,64,256]{2,1,0:T(8,128)(2,1)S(1)}, u32[]{:S(2)}, u32[]{:S(2)}) %collective-permute-start.10) | collective-permute-done | bytes 524320 | tf_op jit(solution)/shard_map/ppermute | solution.py:23
  167.4 3.7 %all_to_all.195 = f32[16,2,128]{2,0,1:T(8,128)S(1)} all-to-all(f32[16,2,128]{2,0,1:T(8,128)S(1)} %fusion.7), channel_id=1, replica_groups=mesh['slab'=2,'col'=4,'row'=2,'ch'=2] {'ch'}, dimensions={1} | all-to-all | bytes 32768 | tf_op jit(solution)/shard_map/all_to_all | solution.py:281
  171.8 4.7 %all_to_all.196 = bf16[16,128,256]{2,0,1:T(8,128)(2,1)S(1)} all-to-all(bf16[16,128,256]{2,0,1:T(8,128)(2,1)S(1)} %copy.200), channel_id=1, replica_groups=mesh['slab'=2,'col'=4,'row'=2,'ch'=2] {'ch'}, dimensions={1} | all-to-all | bytes 2097152 | tf_op jit(solution)/shard_map/all_to_all | solution.py:281
  178.5 4.7 %all_to_all.197 = f32[8,128,256]{2,0,1:T(8,128)S(1)} all-to-all(f32[8,128,256]{2,0,1:T(8,128)S(1)} %copy.204), channel_id=1, replica_groups=mesh['slab'=2,'col'=4,'row'=2,'ch'=2] {'ch'}, dimensions={1} | all-to-all | bytes 2097152 | tf_op jit(solution)/shard_map/all_to_all | solution.py:281
  184.0 4.2 %all_to_all.198 = bf16[8,128,256]{2,0,1:T(8,128)(2,1)S(1)} all-to-all(bf16[8,128,256]{2,0,1:T(8,128)(2,1)S(1)} %copy.202), channel_id=1, replica_groups=mesh['slab'=2,'col'=4,'row'=2,'ch'=2] {'ch'}, dimensions={1} | all-to-all | bytes 1048576 | tf_op jit(solution)/shard_map/all_to_all | solution.py:281
  (157 shorter events, 46.0 us)
Async XLA Ops:
  6.6 17.2 %copy-start = (bf16[2,16,64,256]{3,2,0,1:T(8,128)(2,1)}, bf16[2,16,64,256]{3,2,0,1:T(8,128)(2,1)S(1)}, u32[]{:S(2)}) copy-start(bf16[2,16,64,256]{3,2,0,1:T(8,128)(2,1)S(1)} %copy.175) | copy-start | bytes 3145732
  6.6 17.0 %copy-start.4 = (f32[3,3,32,32]{3,2,1,0:T(8,128)S(1)}, f32[3,3,32,32]{3,2,1,0:T(8,128)}, u32[]{:S(2)}) copy-start(f32[3,3,32,32]{3,2,1,0:T(8,128)} %param.13) | copy-start | bytes 110596
  7.3 11.9 %all-to-all-start.1 = ((f32[2,32,128]{2,0,1:T(2,128)}), f32[2,32,128]{2,0,1:T(2,128)S(1)}, u32[]{:S(2)}, u32[]{:S(2)}) async-start(f32[2,32,128]{2,0,1:T(2,128)} %pad_maximum_fusion.6), calls=%async_computation.1 | async-start | bytes 65536 | tf_op jit(solution)/shard_map/all_to_all | solution.py:281
  10.6 16.7 %collective-permute-start = (bf16[16,64,256]{2,1,0:T(8,128)(2,1)S(1)}, bf16[16,64,256]{2,1,0:T(8,128)(2,1)S(1)}, u32[]{:S(2)}, u32[]{:S(2)}) collective-permute-start(bf16[16,64,256]{2,1,0:T(8,128)(2,1)S(1)} %bitcast.143), channel_id=1, source_target_pairs={{0,4},{4,8},{8,12},{1,5},{5,9},{9,13},{2,6},{6,10},{10,14},{3,7},{... | collective-permute-start | bytes 1572872 | tf_op jit(solution)/shard_map/ppermute | solution.py:23
  19.2 30.5 %all-to-all-start.2 = ((bf16[32,64,256]{2,1,0:T(8,128)(2,1)}), bf16[32,64,256]{2,1,0:T(8,128)(2,1)S(1)}, u32[]{:S(2)}, u32[]{:S(2)}) async-start(bf16[32,64,256]{2,1,0:T(8,128)(2,1)} %param.8), calls=%async_computation.2 | async-start | bytes 2097152 | tf_op jit(solution)/shard_map/all_to_all | solution.py:281
  27.4 16.7 %collective-permute-start.2 = (bf16[8,128,256]{2,1,0:T(8,128)(2,1)S(1)}, bf16[8,128,256]{2,1,0:T(8,128)(2,1)S(1)}, u32[]{:S(2)}, u32[]{:S(2)}) collective-permute-start(bf16[8,128,256]{2,1,0:T(8,128)(2,1)S(1)} %slice.58), channel_id=1, source_target_pairs={{0,4},{4,8},{8,12},{1,5},{5,9},{9,13},{2,6},{6,10},{10,14},{3,7},{... | collective-permute-start | bytes 1572872 | tf_op jit(solution)/shard_map/ppermute | solution.py:23
  33.9 16.9 %copy-start.12 = (f32[1,16,2,128]{3,1,2,0:T(8,128)S(1)}, f32[1,16,2,128]{3,1,2,0:T(8,128)}, u32[]{:S(2)}) copy-start(f32[1,16,2,128]{3,1,2,0:T(8,128)} %get-tuple-element.54) | copy-start | bytes 49156
  33.9 16.9 %copy-start.14 = (f32[1,16,2,128]{3,1,2,0:T(8,128)S(1)}, f32[1,16,2,128]{3,1,2,0:T(8,128)}, u32[]{:S(2)}) copy-start(f32[1,16,2,128]{3,1,2,0:T(8,128)} %get-tuple-element.55) | copy-start | bytes 49156
  33.9 17.1 %copy-start.20 = (bf16[32,32]{1,0:T(8,128)(2,1)S(1)}, bf16[32,32]{1,0:T(8,128)(2,1)}, u32[]{:S(2)}) copy-start(bf16[32,32]{1,0:T(8,128)(2,1)} %subtract_convert_fusion) | copy-start | bytes 6148
  33.9 17.1 %copy-start.21 = (bf16[32,32]{1,0:T(8,128)(2,1)S(1)}, bf16[32,32]{1,0:T(8,128)(2,1)}, u32[]{:S(2)}) copy-start(bf16[32,32]{1,0:T(8,128)(2,1)} %pad_convert_fusion.1) | copy-start | bytes 6148
  34.5 24.7 %collective-permute-start.1 = (bf16[16,64,256]{2,1,0:T(8,128)(2,1)S(1)}, bf16[16,64,256]{2,1,0:T(8,128)(2,1)S(1)}, u32[]{:S(2)}, u32[]{:S(2)}) collective-permute-start(bf16[16,64,256]{2,1,0:T(8,128)(2,1)S(1)} %collective-permute-done), channel_id=1, source_target_pairs={{0,4},{4,8},{8,12},{1,5},{5,9},{9,13},{2,6},{6,10},{10,14},{3,7},{... | collective-permute-start | bytes 1572872 | tf_op jit(solution)/shard_map/ppermute | solution.py:23
  44.1 15.2 %copy-start.2 = (bf16[8,128,256]{2,1,0:T(8,128)(2,1)}, bf16[8,128,256]{2,1,0:T(8,128)(2,1)S(1)}, u32[]{:S(2)}) copy-start(bf16[8,128,256]{2,1,0:T(8,128)(2,1)S(1)} %collective-permute-done.2.mid_ref) | copy-start | bytes 1572868
  44.1 32.0 %collective-permute-start.3 = (bf16[8,128,256]{2,1,0:T(8,128)(2,1)S(1)}, bf16[8,128,256]{2,1,0:T(8,128)(2,1)S(1)}, u32[]{:S(2)}, u32[]{:S(2)}) collective-permute-start(bf16[8,128,256]{2,1,0:T(8,128)(2,1)S(1)} %collective-permute-done.2.mid_ref), channel_id=1, source_target_pairs={{0,4},{4,8},{8,12},{1,5},{5,9},{9,13},{2,6},{6,10},{10,14},{3,7},{... | collective-permute-start | bytes 1572872 | tf_op jit(solution)/shard_map/ppermute | solution.py:23
  88.9 17.3 %copy-start.17 = (f32[1,6336]{1,0:T(1,128)S(1)}, f32[1,6336]{1,0:T(1,128)}, u32[]{:S(2)}) copy-start(f32[1,6336]{1,0:T(1,128)} %and_convert_fusion) | copy-start | bytes 76036
  90.4 3.4 %collective-permute-start.4 = (f32[3,4,256]{2,1,0:T(4,128)S(1)}, f32[3,4,256]{2,1,0:T(4,128)S(1)}, u32[]{:S(2)}, u32[]{:S(2)}) collective-permute-start(f32[3,4,256]{2,1,0:T(4,128)S(1)} %get-tuple-element.52), channel_id=1, source_target_pairs={{0,1},{1,2},{2,3},{4,5},{5,6},{6,7},{8,9},{9,10},{10,11},{12,13},{... | collective-permute-start | bytes 36872 | tf_op jit(solution)/shard_map/ppermute | solution.py:23
  92.4 4.0 %collective-permute-start.5 = (f32[3,4,256]{2,1,0:T(4,128)S(1)}, f32[3,4,256]{2,1,0:T(4,128)S(1)}, u32[]{:S(2)}, u32[]{:S(2)}) collective-permute-start(f32[3,4,256]{2,1,0:T(4,128)S(1)} %get-tuple-element.53), channel_id=1, source_target_pairs={{1,0},{2,1},{3,2},{5,4},{6,5},{7,6},{9,8},{10,9},{11,10},{13,12},{... | collective-permute-start | bytes 36872 | tf_op jit(solution)/shard_map/ppermute | solution.py:23
  96.6 5.8 %collective-permute-start.6 = (f32[3,24,4]{2,1,0:T(8,128)S(1)}, f32[3,24,4]{2,1,0:T(8,128)S(1)}, u32[]{:S(2)}, u32[]{:S(2)}) collective-permute-start(f32[3,24,4]{2,1,0:T(8,128)S(1)} %get-tuple-element.50), channel_id=1, source_target_pairs={{0,4},{4,8},{8,12},{1,5},{5,9},{9,13},{2,6},{6,10},{10,14},{3,7},{... | collective-permute-start | bytes 3464 | tf_op jit(solution)/shard_map/ppermute | solution.py:23
  100.0 5.9 %collective-permute-start.7 = (f32[3,24,4]{2,1,0:T(8,128)S(1)}, f32[3,24,4]{2,1,0:T(8,128)S(1)}, u32[]{:S(2)}, u32[]{:S(2)}) collective-permute-start(f32[3,24,4]{2,1,0:T(8,128)S(1)} %get-tuple-element.51), channel_id=1, source_target_pairs={{4,0},{8,4},{12,8},{5,1},{9,5},{13,9},{6,2},{10,6},{14,10},{7,3},{... | collective-permute-start | bytes 3464 | tf_op jit(solution)/shard_map/ppermute | solution.py:23
  130.1 26.2 %collective-permute-start.8 = (bf16[8,128,256]{2,1,0:T(8,128)(2,1)}, bf16[8,128,256]{2,1,0:T(8,128)(2,1)S(1)}, u32[]{:S(2)}, u32[]{:S(2)}) collective-permute-start(bf16[8,128,256]{2,1,0:T(8,128)(2,1)} %get-tuple-element.35), channel_id=1, source_target_pairs={{4,0},{8,4},{12,8},{5,1},{9,5},{13,9},{6,2},{10,6},{14,10},{7,3},{... | collective-permute-start | bytes 1572872 | tf_op jit(solution)/shard_map/ppermute | solution.py:23
  149.0 17.0 %collective-permute-start.10 = (bf16[16,64,256]{2,1,0:T(8,128)(2,1)S(1)}, bf16[16,64,256]{2,1,0:T(8,128)(2,1)S(1)}, u32[]{:S(2)}, u32[]{:S(2)}) collective-permute-start(bf16[16,64,256]{2,1,0:T(8,128)(2,1)S(1)} %bitcast.144), channel_id=1, source_target_pairs={{4,0},{8,4},{12,8},{5,1},{9,5},{13,9},{6,2},{10,6},{14,10},{7,3},{... | collective-permute-start | bytes 1572872 | tf_op jit(solution)/shard_map/ppermute | solution.py:23
  156.3 14.8 %copy-start.10 = (bf16[8,128,256]{2,1,0:T(8,128)(2,1)S(1)}, bf16[8,128,256]{2,1,0:T(8,128)(2,1)}, u32[]{:S(2)}) copy-start(bf16[8,128,256]{2,1,0:T(8,128)(2,1)} %get-tuple-element.30) | copy-start | bytes 1572868
  156.3 14.8 %copy-start.11 = (bf16[8,128,256]{2,1,0:T(8,128)(2,1)S(1)}, bf16[8,128,256]{2,1,0:T(8,128)(2,1)}, u32[]{:S(2)}) copy-start(bf16[8,128,256]{2,1,0:T(8,128)(2,1)} %get-tuple-element.32) | copy-start | bytes 1572868
  156.5 27.0 %collective-permute-start.9 = (bf16[8,128,256]{2,1,0:T(8,128)(2,1)S(1)}, bf16[8,128,256]{2,1,0:T(8,128)(2,1)S(1)}, u32[]{:S(2)}, u32[]{:S(2)}) collective-permute-start(bf16[8,128,256]{2,1,0:T(8,128)(2,1)S(1)} %add_convert_fusion.1), channel_id=1, source_target_pairs={{4,0},{8,4},{12,8},{5,1},{9,5},{13,9},{6,2},{10,6},{14,10},{7,3},{... | collective-permute-start | bytes 1572872 | tf_op jit(solution)/shard_map/ppermute | solution.py:23
  166.1 22.2 %collective-permute-start.11 = (bf16[16,64,256]{2,1,0:T(8,128)(2,1)S(1)}, bf16[16,64,256]{2,1,0:T(8,128)(2,1)S(1)}, u32[]{:S(2)}, u32[]{:S(2)}) collective-permute-start(bf16[16,64,256]{2,1,0:T(8,128)(2,1)S(1)} %fusion), channel_id=1, source_target_pairs={{4,0},{8,4},{12,8},{5,1},{9,5},{13,9},{6,2},{10,6},{14,10},{7,3},{... | collective-permute-start | bytes 1572872 | tf_op jit(solution)/shard_map/ppermute | solution.py:23
  (15 other events, 122.0 us)

commit v3 on v1

--- a/solution.py
+++ b/solution.py
@@ -13,6 +13,7 @@
 HALO = 4
 LANES = 128
 CHUNKS = 2
+PER_STEP = 4
 VMEM = 56 * 1024 * 1024
 F32, BF16 = jnp.float32, jnp.bfloat16
 
@@ -30,8 +31,8 @@
     return jnp.concatenate([before, shard, after], axis=dim)
 
 
-def band_of(offset, window_refs, tile):
-    window = jnp.concatenate([ref[0] for ref in window_refs], axis=1).astype(F32)
+def band_of(offset, window_refs, tile, slot):
+    window = jnp.concatenate([ref[slot] for ref in window_refs], axis=1).astype(F32)
     span = window.shape[1]
     start = span - tile - DISP - offset
     return pltpu.roll(window, span - start, 1)[:, : tile + DISP].astype(BF16)
@@ -65,65 +66,69 @@
 
 
 def cost_kernel(offset_ref, left_ref, far_ref, mid_ref, near_ref, probs_ref, stats_ref):
-    row = pl.program_id(0)
-    tile = left_ref.shape[2]
-    band = band_of(offset_ref[0], (far_ref, mid_ref, near_ref), tile)
-    products = lax.dot_general(
-        left_ref[0], band, (((0,), (0,)), ((), ())), preferred_element_type=F32
-    )
-    scores = skew_out(products) / math.sqrt(FEAT)
-    exps = jnp.exp(scores - jnp.max(scores, axis=1, keepdims=True))
-    probs = exps / jnp.sum(exps, axis=1, keepdims=True)
-    levels = levels_of(probs.shape)
-    mean = jnp.sum(probs * levels, axis=1, keepdims=True)
-    spread = jnp.sum(probs * (levels - mean) ** 2, axis=1, keepdims=True)
-    probs_ref[0] = probs
+    count, _, tile = left_ref.shape
     lanes = lax.broadcasted_iota(jnp.int32, stats_ref.shape, 1)
 
-    @pl.when(row == 0)
+    @pl.when(pl.program_id(0) == 0)
     def _():
         stats_ref[...] = jnp.zeros_like(stats_ref)
 
-    stats_ref[...] = jnp.where(
-        lanes == row, mean, jnp.where(lanes == row + LANES // 2, spread, stats_ref[...])
-    )
+    stats = stats_ref[...]
+    for slot in range(count):
+        row = pl.program_id(0) * count + slot
+        band = band_of(offset_ref[0], (far_ref, mid_ref, near_ref), tile, slot)
+        products = lax.dot_general(
+            left_ref[slot], band, (((0,), (0,)), ((), ())), preferred_element_type=F32
+        )
+        scores = skew_out(products) / math.sqrt(FEAT)
+        exps = jnp.exp(scores - jnp.max(scores, axis=1, keepdims=True))
+        probs = exps / jnp.sum(exps, axis=1, keepdims=True)
+        levels = levels_of(probs.shape)
+        mean = jnp.sum(probs * levels, axis=1, keepdims=True)
+        spread = jnp.sum(probs * (levels - mean) ** 2, axis=1, keepdims=True)
+        probs_ref[slot] = probs
+        stats = jnp.where(
+            lanes == row, mean, jnp.where(lanes == row + LANES // 2, spread, stats)
+        )
+    stats_ref[...] = stats
 
 
 def grad_kernel(
     base, offset_ref, left_ref, far_ref, mid_ref, near_ref, probs_ref, stats_ref, cots_ref,
     left_out, far_out, mid_out, near_out,
 ):
-    row = pl.program_id(0)
-    tile = left_ref.shape[2]
-    offset = offset_ref[0]
-    band = band_of(offset, (far_ref, mid_ref, near_ref), tile)
-    lanes = lax.broadcasted_iota(jnp.int32, stats_ref.shape, 1)
-
-    def column(ref, index):
-        return jnp.sum(jnp.where(lanes == index, ref[...], 0.0), axis=1, keepdims=True)
-
-    mean = column(stats_ref, row)
-    spread = column(stats_ref, row + LANES // 2)
-    cot_mean = column(cots_ref, row + base)
-    cot_spread = column(cots_ref, row + base + LANES // 2)
-    probs = probs_ref[0]
-    apart = levels_of(probs.shape) - mean
-    grad_scores = probs * (cot_mean * apart + cot_spread * (apart * apart - spread))
-    grad_cost = (grad_scores / math.sqrt(FEAT)).astype(BF16).astype(F32)
-    skewed = skew_in(grad_cost, tile + DISP).astype(BF16)
-    left_grad = lax.dot_general(
-        band, skewed, (((1,), (1,)), ((), ())), preferred_element_type=F32
-    )
-    left_out[0] = left_grad.astype(BF16)
-    right_grad = jnp.dot(left_ref[0], skewed, preferred_element_type=F32)
-    span = 3 * tile
-    padded = jnp.concatenate(
-        [right_grad, jnp.zeros((right_grad.shape[0], span - tile - DISP), F32)], axis=1
-    )
-    moved = pltpu.roll(padded, span - tile - DISP - offset, 1)
-    far_out[0] = moved[:, :tile].astype(BF16)
-    mid_out[0] = moved[:, tile : 2 * tile]
-    near_out[0] = moved[:, 2 * tile :]
+    count, _, tile = left_ref.shape
+    for slot in range(count):
+        row = pl.program_id(0) * count + slot
+        offset = offset_ref[0]
+        band = band_of(offset, (far_ref, mid_ref, near_ref), tile, slot)
+        lanes = lax.broadcasted_iota(jnp.int32, stats_ref.shape, 1)
+
+        def column(ref, index):
+            return jnp.sum(jnp.where(lanes == index, ref[...], 0.0), axis=1, keepdims=True)
+
+        mean = column(stats_ref, row)
+        spread = column(stats_ref, row + LANES // 2)
+        cot_mean = column(cots_ref, row + base)
+        cot_spread = column(cots_ref, row + base + LANES // 2)
+        probs = probs_ref[slot]
+        apart = levels_of(probs.shape) - mean
+        grad_scores = probs * (cot_mean * apart + cot_spread * (apart * apart - spread))
+        grad_cost = (grad_scores / math.sqrt(FEAT)).astype(BF16).astype(F32)
+        skewed = skew_in(grad_cost, tile + DISP).astype(BF16)
+        left_grad = lax.dot_general(
+            band, skewed, (((1,), (1,)), ((), ())), preferred_element_type=F32
+        )
+        left_out[slot] = left_grad.astype(BF16)
+        right_grad = jnp.dot(left_ref[slot], skewed, preferred_element_type=F32)
+        span = 3 * tile
+        padded = jnp.concatenate(
+            [right_grad, jnp.zeros((right_grad.shape[0], span - tile - DISP), F32)], axis=1
+        )
+        moved = pltpu.roll(padded, span - tile - DISP - offset, 1)
+        far_out[slot] = moved[:, :tile].astype(BF16)
+        mid_out[slot] = moved[:, tile : 2 * tile]
+        near_out[slot] = moved[:, 2 * tile :]
 
 
 def split_halves(values):
@@ -222,8 +227,12 @@
     return out[:3, :cells].reshape(3, rows, cols)
 
 
-def row_block(array, base=0):
-    return pl.BlockSpec((1,) + array.shape[1:], lambda row: (row + base, 0, 0))
+def per_step(rows):
+    return math.gcd(rows, PER_STEP)
+
+
+def row_block(array, per, base=0):
+    return pl.BlockSpec((per,) + array.shape[1:], lambda row: (row + base // per, 0, 0))
 
 
 def whole_block(shape):
@@ -241,14 +250,15 @@
 def match(offsets, left, base, window):
     tile = left.shape[2]
     rows = window[0].shape[0]
+    per = per_step(rows)
     probs = jax.ShapeDtypeStruct((rows, tile, DISP), F32)
     stats = jax.ShapeDtypeStruct((tile, LANES), F32)
     return pl.pallas_call(
         cost_kernel,
-        grid=(rows,),
-        in_specs=[pl.BlockSpec(memory_space=pltpu.SMEM), row_block(left, base)]
-        + [row_block(part) for part in window],
-        out_specs=[row_block(probs), whole_block(stats.shape)],
+        grid=(rows // per,),
+        in_specs=[pl.BlockSpec(memory_space=pltpu.SMEM), row_block(left, per, base)]
+        + [row_block(part, per) for part in window],
+        out_specs=[row_block(probs, per), whole_block(stats.shape)],
         out_shape=[probs, stats],
         compiler_params=pltpu.CompilerParams(vmem_limit_bytes=VMEM),
         cost_estimate=cost_of(rows, tile),
@@ -259,15 +269,16 @@
 def match_grads(offsets, left, base, window, probs, stats, cots):
     feats, tile = left.shape[1:]
     rows = window[0].shape[0]
+    per = per_step(rows)
     narrow = jax.ShapeDtypeStruct((rows, feats, tile), BF16)
     wide = jax.ShapeDtypeStruct((rows, feats, tile), F32)
     return pl.pallas_call(
         functools.partial(grad_kernel, base),
-        grid=(rows,),
-        in_specs=[pl.BlockSpec(memory_space=pltpu.SMEM), row_block(left, base)]
-        + [row_block(part) for part in window]
-        + [row_block(probs), whole_block(stats.shape), whole_block(cots.shape)],
-        out_specs=[row_block(narrow)] * 4,
+        grid=(rows // per,),
+        in_specs=[pl.BlockSpec(memory_space=pltpu.SMEM), row_block(left, per, base)]
+        + [row_block(part, per) for part in window]
+        + [row_block(probs, per), whole_block(stats.shape), whole_block(cots.shape)],
+        out_specs=[row_block(narrow, per)] * 4,
         out_shape=[narrow, narrow, wide, wide],
         compiler_params=pltpu.CompilerParams(vmem_limit_bytes=VMEM),
         cost_estimate=cost_of(rows, tile),
@@ -292,7 +303,11 @@
     chunks = chunk_count(rows)
     step = rows // chunks
     near = [whole_near[index * step : (index + 1) * step] for index in range(chunks)]
-    mid = [from_behind(part, "col", 1) for part in near]
+    mid = []
+    for index in range(chunks):
+        if mid:
+            mid[-1], near[index] = lax.optimization_barrier((mid[-1], near[index]))
+        mid.append(from_behind(near[index], "col", 1))
     left = to_rows(left_feat, 0, 1)
     keep_cols = valid.astype(F32)
     planes = to_rows(jnp.stack([keep_cols, grad_out * keep_cols]), 1, 2)

time: 188 us -> 185 us (0.984)
  other arithmetic: 12.1 us -> 10 us
  waiting for transfers between devices: 37.9 us -> 35.9 us
  Pallas kernels: 56 us -> 57.9 us
    ppermute x12, waiting for transfers between devices: 37.9 us -> 35.9 us  [from_behind(): lax.ppermute(value, axis, [(source, source + steps) for source in range(f...]
    pallas_call x4, Pallas kernels: 46.3 us -> 48.2 us  [the longest x2 24.3 us: match(): pl.pallas_call(cost_kernel, grid=(rows // per,), in_specs=[pl.BlockSpec(m...]
  transfers between devices with their start and end apart: 15 -> 15, of which waited for: 7 -> 8; matrix products, arithmetic and copies ran while one was open for 10% -> 8% of each run, Pallas kernels for 12% -> 13%
where the time goes in v3:
time: 185 us; the launch traced here: 183 us
  Pallas kernels  57.9 us (31%)
  starting transfers between devices  42.5 us (23%)
  waiting for transfers between devices  35.9 us (19%)
  blocking collectives  21.9 us (12%)
  local copies, waits for them, and re-layouts  12.9 us (7%)
  other arithmetic  10 us (5%)
  between operations  1.92 us (1%)
    ppermute x12, waiting for transfers between devices, from_behind(): lax.ppermute(value, axis, [(source, source + steps) for source in range(f...  35.9 us
    ppermute x12, starting transfers between devices, from_behind(): lax.ppermute(value, axis, [(source, source + steps) for source in range(f...  32.2 us
    pallas_call x2, Pallas kernels, match(): pl.pallas_call(cost_kernel, grid=(rows // per,), in_specs=[pl.BlockSpec(m...  24.3 us
    pallas_call x2, Pallas kernels, match_grads(): pl.pallas_call(functools.partial(grad_kernel, base), grid=(rows // per,),...  23.9 us
    all_to_all x5, blocking collectives, to_rows(): return lax.all_to_all(array, 'ch', rows_dim, other_dim, tiled=True)  21.9 us
    all_to_all x3, starting transfers between devices, to_rows(): return lax.all_to_all(array, 'ch', rows_dim, other_dim, tiled=True)  10.3 us
    pallas_call x1, Pallas kernels, refine(): pl.pallas_call(functools.partial(refine_kernel, cols), out_shape=jax.Shap...  9.71 us
  transfers between devices with their start and end apart: 15, of which 8 were waited for; matrix products, arithmetic and copies ran while one was open for 8% of the time, Pallas kernels for 13%

profile of v3, /device:TPU:0, one launch (start us, length us, event | category | flops | bytes accessed | tf_op | source)
XLA Modules:
  0.0 183.1 jit_solution(11481465568841223016)
XLA Ops:
  0.7 5.7 %all_to_all.127 = bf16[32,64,256]{2,1,0:T(8,128)(2,1)S(1)} all-to-all(bf16[32,64,256]{2,1,0:T(8,128)(2,1)} %param.9), channel_id=1, replica_groups=mesh['slab'=2,'col'=4,'row'=2,'ch'=2] {'ch'}, dimensions={0} | all-to-all | bytes 2097152 | tf_op jit(solution)/shard_map/all_to_all | solution.py:290
  7.1 3.3 %all-to-all-start.1 = ((f32[2,32,128]{2,0,1:T(2,128)}), f32[2,32,128]{2,0,1:T(2,128)S(1)}, u32[]{:S(2)}, u32[]{:S(2)}) async-start(f32[2,32,128]{2,0,1:T(2,128)} %pad_maximum_fusion.6), calls=%async_computation.1 | async-start | bytes 65536 | tf_op jit(solution)/shard_map/all_to_all | solution.py:290
  10.5 5.0 %collective-permute-start = (bf16[8,128,256]{2,1,0:T(8,128)(2,1)S(1)}, bf16[8,128,256]{2,1,0:T(8,128)(2,1)S(1)}, u32[]{:S(2)}, u32[]{:S(2)}) collective-permute-start(bf16[8,128,256]{2,1,0:T(8,128)(2,1)S(1)} %get-tuple-element.40.near_ref), channel_id=1, source_target_pairs={{0,4},{4,8},{8,12},{1,5},{5,9},{9,13},{2,6},{6,10},{10,14},{3,7},{... | collective-permute-start | bytes 1572872 | tf_op jit(solution)/shard_map/ppermute | solution.py:24
  18.0 3.6 %all-to-all-start.2 = ((bf16[32,64,256]{2,1,0:T(8,128)(2,1)}), bf16[32,64,256]{2,1,0:T(8,128)(2,1)S(1)}, u32[]{:S(2)}, u32[]{:S(2)}) async-start(bf16[32,64,256]{2,1,0:T(8,128)(2,1)} %param.8), calls=%async_computation.2 | async-start | bytes 2097152 | tf_op jit(solution)/shard_map/all_to_all | solution.py:290
  23.6 3.7 %collective-permute-done.mid_ref = bf16[8,128,256]{2,1,0:T(8,128)(2,1)S(1)} collective-permute-done((bf16[8,128,256]{2,1,0:T(8,128)(2,1)S(1)}, bf16[8,128,256]{2,1,0:T(8,128)(2,1)S(1)}, u32[]{:S(2)}, u32[]{:S(2)}) %collective-permute-start) | collective-permute-done | bytes 524320 | tf_op jit(solution)/shard_map/ppermute | solution.py:24
  27.2 5.2 %collective-permute-start.2 = (bf16[8,128,256]{2,1,0:T(8,128)(2,1)S(1)}, bf16[8,128,256]{2,1,0:T(8,128)(2,1)}, u32[]{:S(2)}, u32[]{:S(2)}) collective-permute-start(bf16[8,128,256]{2,1,0:T(8,128)(2,1)S(1)} %get-tuple-element.27.near_ref), channel_id=1, source_target_pairs={{0,4},{4,8},{8,12},{1,5},{5,9},{9,13},{2,6},{6,10},{10,14},{3,7},{... | collective-permute-start | bytes 1572872 | tf_op jit(solution)/shard_map/ppermute | solution.py:24
  33.7 2.9 %collective-permute-start.1 = (bf16[8,128,256]{2,1,0:T(8,128)(2,1)S(1)}, bf16[8,128,256]{2,1,0:T(8,128)(2,1)S(1)}, u32[]{:S(2)}, u32[]{:S(2)}) collective-permute-start(bf16[8,128,256]{2,1,0:T(8,128)(2,1)S(1)} %collective-permute-done.mid_ref), channel_id=1, source_target_pairs={{0,4},{4,8},{8,12},{1,5},{5,9},{9,13},{2,6},{6,10},{10,14},{3,7},{... | collective-permute-start | bytes 1572872 | tf_op jit(solution)/shard_map/ppermute | solution.py:24
  36.6 7.3 %collective-permute-done.2.mid_ref = bf16[8,128,256]{2,1,0:T(8,128)(2,1)} collective-permute-done((bf16[8,128,256]{2,1,0:T(8,128)(2,1)S(1)}, bf16[8,128,256]{2,1,0:T(8,128)(2,1)}, u32[]{:S(2)}, u32[]{:S(2)}) %collective-permute-start.2) | collective-permute-done | bytes 524320 | tf_op jit(solution)/shard_map/ppermute | solution.py:24
  44.0 5.3 %collective-permute-start.3 = (bf16[8,128,256]{2,1,0:T(8,128)(2,1)}, bf16[8,128,256]{2,1,0:T(8,128)(2,1)}, u32[]{:S(2)}, u32[]{:S(2)}) collective-permute-start(bf16[8,128,256]{2,1,0:T(8,128)(2,1)} %collective-permute-done.2.mid_ref), channel_id=1, source_target_pairs={{0,4},{4,8},{8,12},{1,5},{5,9},{9,13},{2,6},{6,10},{10,14},{3,7},{... | collective-permute-start | bytes 1572872 | tf_op jit(solution)/shard_map/ppermute | solution.py:24
  56.0 12.1 %match.2 = (f32[8,256,256]{2,1,0:T(8,128)}, f32[256,128]{1,0:T(8,128)}) custom-call(s32[1]{0:T(128)S(6)} %copy.157.offset_ref, bf16[16,128,256]{2,1,0:T(8,128)(2,1)} %bitcast.93, bf16[8,128,256]{2,1,0:T(8,128)(2,1)} %copy-done.3, bf16[8,128,256]{2,1,0:T(8,128)(2,1)} %copy-done.2, bf16[8,128,256]{2,1,0:T(8,128)(2,1)} %copy-done), custom_call_target="tpu_custom_call" | custom-call | flops 402653184 | bytes 33554432 | tf_op jit(solution)/shard_map/match/pallas_call | solution.py:256
  68.2 12.2 %match.3 = (f32[8,256,256]{2,1,0:T(8,128)}, f32[256,128]{1,0:T(8,128)}) custom-call(s32[1]{0:T(128)S(6)} %copy.157.offset_ref, bf16[16,128,256]{2,1,0:T(8,128)(2,1)} %bitcast.94, bf16[8,128,256]{2,1,0:T(8,128)(2,1)} %collective-permute-done.3.far_ref, bf16[8,128,256]{2,1,0:T(8,128)(2,1)} %collective-permute-done.2.mid_ref, bf16[8,128,256]{2,1,0:T(8,128)(2,1)} %copy-done.1), custom_call_target="tpu_custom_call" | custom-call | flops 402653184 | bytes 33554432 | tf_op jit(solution)/shard_map/match/pallas_call | solution.py:256
  84.4 3.5 %collective-permute-done.5 = f32[3,4,256]{2,1,0:T(4,128)S(1)} collective-permute-done((f32[3,4,256]{2,1,0:T(4,128)S(1)}, f32[3,4,256]{2,1,0:T(4,128)S(1)}, u32[]{:S(2)}, u32[]{:S(2)}) %collective-permute-start.5) | collective-permute-done | bytes 12320 | tf_op jit(solution)/shard_map/ppermute | solution.py:24
  88.0 4.4 %collective-permute-start.6 = (f32[3,24,4]{2,1,0:T(8,128)S(1)}, f32[3,24,4]{2,1,0:T(8,128)S(1)}, u32[]{:S(2)}, u32[]{:S(2)}) collective-permute-start(f32[3,24,4]{2,1,0:T(8,128)S(1)} %get-tuple-element.52), channel_id=1, source_target_pairs={{0,4},{4,8},{8,12},{1,5},{5,9},{9,13},{2,6},{6,10},{10,14},{3,7},{... | collective-permute-start | bytes 3464 | tf_op jit(solution)/shard_map/ppermute | solution.py:24
  94.8 3.5 %collective-permute-done.7 = f32[3,24,4]{2,1,0:T(8,128)S(1)} collective-permute-done((f32[3,24,4]{2,1,0:T(8,128)S(1)}, f32[3,24,4]{2,1,0:T(8,128)S(1)}, u32[]{:S(2)}, u32[]{:S(2)}) %collective-permute-start.7) | collective-permute-done | bytes 1184 | tf_op jit(solution)/shard_map/ppermute | solution.py:24
  99.3 9.7 %refine.1 = f32[8,6400]{1,0:T(8,128)} custom-call(f32[8,6400]{1,0:T(8,128)} %select_maximum_fusion.fields_ref, bf16[32,96]{1,0:T(8,128)(2,1)} %get-tuple-element.63.first_ref, bf16[288,96]{1,0:T(8,128)(2,1)} %get-tuple-element.61.middle_ref, bf16[16,96]{1,0:T(8,128)(2,1)} %pad_maximum_fusion.13.last_ref, bf16[32,96]{1,0:T(8,128)(2,1)} %get-tuple-element.64.last_back_ref, ...), custom_call_target="tpu_custom_call" | custom-call | tf_op jit(solution)/shard_map/refine/pallas_call | solution.py:213
  111.3 11.9 %match_grads.3 = (bf16[8,128,256]{2,1,0:T(8,128)(2,1)}, bf16[8,128,256]{2,1,0:T(8,128)(2,1)}, f32[8,128,256]{2,1,0:T(8,128)}, f32[8,128,256]{2,1,0:T(8,128)}) custom-call(s32[1]{0:T(128)S(6)} %copy.157.offset_ref, bf16[16,128,256]{2,1,0:T(8,128)(2,1)} %bitcast.95, bf16[8,128,256]{2,1,0:T(8,128)(2,1)} %collective-permute-done.3.far_ref, ...), custom_call_target="tpu_custom_call" | custom-call | flops 402653184 | bytes 33554432 | tf_op jit(solution)/shard_map/match_grads/pallas_call | solution.py:275
  124.5 12.0 %match_grads.2 = (bf16[8,128,256]{2,1,0:T(8,128)(2,1)}, bf16[8,128,256]{2,1,0:T(8,128)(2,1)}, f32[8,128,256]{2,1,0:T(8,128)}, f32[8,128,256]{2,1,0:T(8,128)}) custom-call(s32[1]{0:T(128)S(6)} %copy.157.offset_ref, bf16[16,128,256]{2,1,0:T(8,128)(2,1)} %bitcast.96, bf16[8,128,256]{2,1,0:T(8,128)(2,1)} %copy-done.3, bf16[8,128,256]{2,1,0:T(8,128)(2,1)} %copy-done.2, ...), custom_call_target="tpu_custom_call" | custom-call | flops 402653184 | bytes 33554432 | tf_op jit(solution)/shard_map/match_grads/pallas_call | solution.py:275
  141.6 12.5 %collective-permute-done.8 = bf16[8,128,256]{2,1,0:T(8,128)(2,1)S(1)} collective-permute-done((bf16[8,128,256]{2,1,0:T(8,128)(2,1)}, bf16[8,128,256]{2,1,0:T(8,128)(2,1)S(1)}, u32[]{:S(2)}, u32[]{:S(2)}) %collective-permute-start.8) | collective-permute-done | bytes 524320 | tf_op jit(solution)/shard_map/ppermute | solution.py:24
  155.6 3.7 %all_to_all.128 = f32[16,2,128]{2,0,1:T(8,128)S(1)} all-to-all(f32[16,2,128]{2,0,1:T(8,128)S(1)} %fusion.5), channel_id=1, replica_groups=mesh['slab'=2,'col'=4,'row'=2,'ch'=2] {'ch'}, dimensions={1} | all-to-all | bytes 32768 | tf_op jit(solution)/shard_map/all_to_all | solution.py:290
  159.9 4.2 %all_to_all.129 = bf16[8,128,256]{2,0,1:T(8,128)(2,1)S(1)} all-to-all(bf16[8,128,256]{2,0,1:T(8,128)(2,1)S(1)} %copy.144), channel_id=1, replica_groups=mesh['slab'=2,'col'=4,'row'=2,'ch'=2] {'ch'}, dimensions={1} | all-to-all | bytes 1048576 | tf_op jit(solution)/shard_map/all_to_all | solution.py:290
  164.1 4.1 %all_to_all.130 = bf16[8,128,256]{2,0,1:T(8,128)(2,1)S(1)} all-to-all(bf16[8,128,256]{2,0,1:T(8,128)(2,1)S(1)} %copy.143), channel_id=1, replica_groups=mesh['slab'=2,'col'=4,'row'=2,'ch'=2] {'ch'}, dimensions={1} | all-to-all | bytes 1048576 | tf_op jit(solution)/shard_map/all_to_all | solution.py:290
  170.7 3.5 %all-to-all-start.7 = ((bf16[8,128,256]{2,0,1:T(8,128)(2,1)}), bf16[8,128,256]{2,0,1:T(8,128)(2,1)S(1)}, u32[]{:S(2)}, u32[]{:S(2)}) async-start(bf16[8,128,256]{2,0,1:T(8,128)(2,1)} %copy.147), calls=%async_computation.7 | async-start | bytes 1048576 | tf_op jit(solution)/shard_map/all_to_all | solution.py:290
  174.2 2.4 %collective-permute-done.9 = bf16[8,128,256]{2,1,0:T(8,128)(2,1)S(1)} collective-permute-done((bf16[8,128,256]{2,1,0:T(8,128)(2,1)S(1)}, bf16[8,128,256]{2,1,0:T(8,128)(2,1)S(1)}, u32[]{:S(2)}, u32[]{:S(2)}) %collective-permute-start.9) | collective-permute-done | bytes 524320 | tf_op jit(solution)/shard_map/ppermute | solution.py:24
  177.0 4.2 %all_to_all.131 = bf16[8,128,256]{2,0,1:T(8,128)(2,1)S(1)} all-to-all(bf16[8,128,256]{2,0,1:T(8,128)(2,1)S(1)} %copy.146), channel_id=1, replica_groups=mesh['slab'=2,'col'=4,'row'=2,'ch'=2] {'ch'}, dimensions={1} | all-to-all | bytes 1048576 | tf_op jit(solution)/shard_map/all_to_all | solution.py:290
  (143 shorter events, 35.5 us)
Async XLA Ops:
  7.1 10.8 %all-to-all-start.1 = ((f32[2,32,128]{2,0,1:T(2,128)}), f32[2,32,128]{2,0,1:T(2,128)S(1)}, u32[]{:S(2)}, u32[]{:S(2)}) async-start(f32[2,32,128]{2,0,1:T(2,128)} %pad_maximum_fusion.6), calls=%async_computation.1 | async-start | bytes 65536 | tf_op jit(solution)/shard_map/all_to_all | solution.py:290
  10.5 41.1 %copy-start = (bf16[8,128,256]{2,1,0:T(8,128)(2,1)}, bf16[8,128,256]{2,1,0:T(8,128)(2,1)S(1)}, u32[]{:S(2)}) copy-start(bf16[8,128,256]{2,1,0:T(8,128)(2,1)S(1)} %get-tuple-element.40.near_ref) | copy-start | bytes 1572868
  10.5 41.1 %copy-start.1 = (bf16[8,128,256]{2,1,0:T(8,128)(2,1)}, bf16[8,128,256]{2,1,0:T(8,128)(2,1)S(1)}, u32[]{:S(2)}) copy-start(bf16[8,128,256]{2,1,0:T(8,128)(2,1)S(1)} %get-tuple-element.27.near_ref) | copy-start | bytes 1572868
  10.5 16.7 %collective-permute-start = (bf16[8,128,256]{2,1,0:T(8,128)(2,1)S(1)}, bf16[8,128,256]{2,1,0:T(8,128)(2,1)S(1)}, u32[]{:S(2)}, u32[]{:S(2)}) collective-permute-start(bf16[8,128,256]{2,1,0:T(8,128)(2,1)S(1)} %get-tuple-element.40.near_ref), channel_id=1, source_target_pairs={{0,4},{4,8},{8,12},{1,5},{5,9},{9,13},{2,6},{6,10},{10,14},{3,7},{... | collective-permute-start | bytes 1572872 | tf_op jit(solution)/shard_map/ppermute | solution.py:24
  18.0 32.6 %all-to-all-start.2 = ((bf16[32,64,256]{2,1,0:T(8,128)(2,1)}), bf16[32,64,256]{2,1,0:T(8,128)(2,1)S(1)}, u32[]{:S(2)}, u32[]{:S(2)}) async-start(bf16[32,64,256]{2,1,0:T(8,128)(2,1)} %param.8), calls=%async_computation.2 | async-start | bytes 2097152 | tf_op jit(solution)/shard_map/all_to_all | solution.py:290
  27.2 28.0 %copy-start.2 = (bf16[8,128,256]{2,1,0:T(8,128)(2,1)}, bf16[8,128,256]{2,1,0:T(8,128)(2,1)S(1)}, u32[]{:S(2)}) copy-start(bf16[8,128,256]{2,1,0:T(8,128)(2,1)S(1)} %collective-permute-done.mid_ref) | copy-start | bytes 1572868
  27.2 16.7 %collective-permute-start.2 = (bf16[8,128,256]{2,1,0:T(8,128)(2,1)S(1)}, bf16[8,128,256]{2,1,0:T(8,128)(2,1)}, u32[]{:S(2)}, u32[]{:S(2)}) collective-permute-start(bf16[8,128,256]{2,1,0:T(8,128)(2,1)S(1)} %get-tuple-element.27.near_ref), channel_id=1, source_target_pairs={{0,4},{4,8},{8,12},{1,5},{5,9},{9,13},{2,6},{6,10},{10,14},{3,7},{... | collective-permute-start | bytes 1572872 | tf_op jit(solution)/shard_map/ppermute | solution.py:24
  33.7 19.5 %copy-start.12 = (bf16[288,32]{1,0:T(8,128)(2,1)S(1)}, bf16[288,32]{1,0:T(8,128)(2,1)}, u32[]{:S(2)}) copy-start(bf16[288,32]{1,0:T(8,128)(2,1)} %bitcast_convert_fusion.1) | copy-start | bytes 55300
  33.7 21.4 %collective-permute-start.1 = (bf16[8,128,256]{2,1,0:T(8,128)(2,1)S(1)}, bf16[8,128,256]{2,1,0:T(8,128)(2,1)S(1)}, u32[]{:S(2)}, u32[]{:S(2)}) collective-permute-start(bf16[8,128,256]{2,1,0:T(8,128)(2,1)S(1)} %collective-permute-done.mid_ref), channel_id=1, source_target_pairs={{0,4},{4,8},{8,12},{1,5},{5,9},{9,13},{2,6},{6,10},{10,14},{3,7},{... | collective-permute-start | bytes 1572872 | tf_op jit(solution)/shard_map/ppermute | solution.py:24
  44.0 24.2 %collective-permute-start.3 = (bf16[8,128,256]{2,1,0:T(8,128)(2,1)}, bf16[8,128,256]{2,1,0:T(8,128)(2,1)}, u32[]{:S(2)}, u32[]{:S(2)}) collective-permute-start(bf16[8,128,256]{2,1,0:T(8,128)(2,1)} %collective-permute-done.2.mid_ref), channel_id=1, source_target_pairs={{0,4},{4,8},{8,12},{1,5},{5,9},{9,13},{2,6},{6,10},{10,14},{3,7},{... | collective-permute-start | bytes 1572872 | tf_op jit(solution)/shard_map/ppermute | solution.py:24
  68.1 25.8 %copy-start.21 = (bf16[16,32]{1,0:T(8,128)(2,1)S(1)}, bf16[16,32]{1,0:T(8,128)(2,1)}, u32[]{:S(2)}) copy-start(bf16[16,32]{1,0:T(8,128)(2,1)} %subtract_convert_fusion.2) | copy-start | bytes 3076
  68.1 26.4 %copy-start.16 = (f32[1,16,2,128]{3,1,2,0:T(8,128)S(1)}, f32[1,16,2,128]{3,1,2,0:T(8,128)}, u32[]{:S(2)}) copy-start(f32[1,16,2,128]{3,1,2,0:T(8,128)} %get-tuple-element.57) | copy-start | bytes 49156
  68.2 26.5 %copy-start.14 = (f32[1,16,2,128]{3,1,2,0:T(8,128)S(1)}, f32[1,16,2,128]{3,1,2,0:T(8,128)}, u32[]{:S(2)}) copy-start(f32[1,16,2,128]{3,1,2,0:T(8,128)} %get-tuple-element.56) | copy-start | bytes 49156
  81.8 2.6 %collective-permute-start.4 = (f32[3,4,256]{2,1,0:T(4,128)S(1)}, f32[3,4,256]{2,1,0:T(4,128)S(1)}, u32[]{:S(2)}, u32[]{:S(2)}) collective-permute-start(f32[3,4,256]{2,1,0:T(4,128)S(1)} %get-tuple-element.54), channel_id=1, source_target_pairs={{0,1},{1,2},{2,3},{4,5},{5,6},{6,7},{8,9},{9,10},{10,11},{12,13},{... | collective-permute-start | bytes 36872 | tf_op jit(solution)/shard_map/ppermute | solution.py:24
  83.1 4.8 %collective-permute-start.5 = (f32[3,4,256]{2,1,0:T(4,128)S(1)}, f32[3,4,256]{2,1,0:T(4,128)S(1)}, u32[]{:S(2)}, u32[]{:S(2)}) collective-permute-start(f32[3,4,256]{2,1,0:T(4,128)S(1)} %get-tuple-element.55), channel_id=1, source_target_pairs={{1,0},{2,1},{3,2},{5,4},{6,5},{7,6},{9,8},{10,9},{11,10},{13,12},{... | collective-permute-start | bytes 36872 | tf_op jit(solution)/shard_map/ppermute | solution.py:24
  88.0 6.8 %collective-permute-start.6 = (f32[3,24,4]{2,1,0:T(8,128)S(1)}, f32[3,24,4]{2,1,0:T(8,128)S(1)}, u32[]{:S(2)}, u32[]{:S(2)}) collective-permute-start(f32[3,24,4]{2,1,0:T(8,128)S(1)} %get-tuple-element.52), channel_id=1, source_target_pairs={{0,4},{4,8},{8,12},{1,5},{5,9},{9,13},{2,6},{6,10},{10,14},{3,7},{... | collective-permute-start | bytes 3464 | tf_op jit(solution)/shard_map/ppermute | solution.py:24
  92.4 5.9 %collective-permute-start.7 = (f32[3,24,4]{2,1,0:T(8,128)S(1)}, f32[3,24,4]{2,1,0:T(8,128)S(1)}, u32[]{:S(2)}, u32[]{:S(2)}) collective-permute-start(f32[3,24,4]{2,1,0:T(8,128)S(1)} %get-tuple-element.53), channel_id=1, source_target_pairs={{4,0},{8,4},{12,8},{5,1},{9,5},{13,9},{6,2},{10,6},{14,10},{7,3},{... | collective-permute-start | bytes 3464 | tf_op jit(solution)/shard_map/ppermute | solution.py:24
  123.2 16.9 %collective-permute-start.10 = (bf16[8,128,256]{2,1,0:T(8,128)(2,1)}, bf16[8,128,256]{2,1,0:T(8,128)(2,1)S(1)}, u32[]{:S(2)}, u32[]{:S(2)}) collective-permute-start(bf16[8,128,256]{2,1,0:T(8,128)(2,1)} %get-tuple-element.38), channel_id=1, source_target_pairs={{4,0},{8,4},{12,8},{5,1},{9,5},{13,9},{6,2},{10,6},{14,10},{7,3},{... | collective-permute-start | bytes 1572872 | tf_op jit(solution)/shard_map/ppermute | solution.py:24
  136.5 17.6 %collective-permute-start.8 = (bf16[8,128,256]{2,1,0:T(8,128)(2,1)}, bf16[8,128,256]{2,1,0:T(8,128)(2,1)S(1)}, u32[]{:S(2)}, u32[]{:S(2)}) collective-permute-start(bf16[8,128,256]{2,1,0:T(8,128)(2,1)} %get-tuple-element.35), channel_id=1, source_target_pairs={{4,0},{8,4},{12,8},{5,1},{9,5},{13,9},{6,2},{10,6},{14,10},{7,3},{... | collective-permute-start | bytes 1572872 | tf_op jit(solution)/shard_map/ppermute | solution.py:24
  140.0 19.3 %copy-start.11 = (bf16[8,128,256]{2,1,0:T(8,128)(2,1)S(1)}, bf16[8,128,256]{2,1,0:T(8,128)(2,1)}, u32[]{:S(2)}) copy-start(bf16[8,128,256]{2,1,0:T(8,128)(2,1)} %get-tuple-element.30) | copy-start | bytes 1572868
  140.1 19.5 %copy-start.10 = (bf16[8,128,256]{2,1,0:T(8,128)(2,1)S(1)}, bf16[8,128,256]{2,1,0:T(8,128)(2,1)}, u32[]{:S(2)}) copy-start(bf16[8,128,256]{2,1,0:T(8,128)(2,1)} %get-tuple-element.32) | copy-start | bytes 1572868
  140.2 29.4 %collective-permute-start.11 = (bf16[8,128,256]{2,1,0:T(8,128)(2,1)S(1)}, bf16[8,128,256]{2,1,0:T(8,128)(2,1)S(1)}, u32[]{:S(2)}, u32[]{:S(2)}) collective-permute-start(bf16[8,128,256]{2,1,0:T(8,128)(2,1)S(1)} %add_convert_fusion.1), channel_id=1, source_target_pairs={{4,0},{8,4},{12,8},{5,1},{9,5},{13,9},{6,2},{10,6},{14,10},{7,3},{... | collective-permute-start | bytes 1572872 | tf_op jit(solution)/shard_map/ppermute | solution.py:24
  154.3 22.3 %collective-permute-start.9 = (bf16[8,128,256]{2,1,0:T(8,128)(2,1)S(1)}, bf16[8,128,256]{2,1,0:T(8,128)(2,1)S(1)}, u32[]{:S(2)}, u32[]{:S(2)}) collective-permute-start(bf16[8,128,256]{2,1,0:T(8,128)(2,1)S(1)} %add_convert_fusion.3), channel_id=1, source_target_pairs={{4,0},{8,4},{12,8},{5,1},{9,5},{13,9},{6,2},{10,6},{14,10},{7,3},{... | collective-permute-start | bytes 1572872 | tf_op jit(solution)/shard_map/ppermute | solution.py:24
  170.7 6.3 %all-to-all-start.7 = ((bf16[8,128,256]{2,0,1:T(8,128)(2,1)}), bf16[8,128,256]{2,0,1:T(8,128)(2,1)S(1)}, u32[]{:S(2)}, u32[]{:S(2)}) async-start(bf16[8,128,256]{2,0,1:T(8,128)(2,1)} %copy.147), calls=%async_computation.7 | async-start | bytes 1048576 | tf_op jit(solution)/shard_map/all_to_all | solution.py:290
  (14 other events, 117.4 us)
